TPU v7x, 256 devices: a whole 4x4x8 slice. The times are simulated.
256 devices in a mesh: gx: 8 (over y, z_hi), gy: 4 (over x), gz: 8 (over z_lo, core).
Axes of the slice: x: 4, y: 4, z: 8 (z_hi: 2, z_lo: 4; z = z_hi * 4 + z_lo), core: 2. Of those that a mesh axis runs over, the one named last changes fastest.
Arguments:
- base_flow: float32 [3, 64, 128, 1024], P(None, 'gx', 'gy', 'gz'), may hold values from -4 to 4
- adjoint_velocity: float32 [3, 64, 128, 1024], P(None, 'gx', 'gy', 'gz'), may hold values from -3.6 to 3.6
- penalty: float32 [64, 128, 1024], P('gx', 'gy', 'gz'), may hold values from 4 to 64
Outputs:
- projected: float32 [3, 64, 128, 1024], P(None, 'gx', 'gy', 'gz')
- pressure: float32 [64, 128, 1024], P('gx', 'gy', 'gz')
All inputs are finite; a program needn't handle non-finite values.
Results may differ from a plain program's by a relative error of at most 0.00013.
Values sent between devices are 32-bit elements; how exact they have to be, the bound alone decides.
A program may use at most 64 MiB of HBM per device.

v0:
```python
import jax
import jax.numpy as jnp
import numpy as np
from jax import lax
from jax.sharding import PartitionSpec as P

ITERS = 3


def with_halo(cells, sides, width, closed):
    for axis, dim in sides:
        count = lax.axis_size(axis)
        ends = count if closed else count - 1
        head = lax.slice_in_dim(cells, 0, width, axis=dim)
        tail = lax.slice_in_dim(cells, cells.shape[dim] - width, cells.shape[dim], axis=dim)
        cells = jnp.concatenate(
            [
                lax.ppermute(tail, axis, [(i, (i + 1) % count) for i in range(ends)]),
                cells,
                lax.ppermute(head, axis, [((i + 1) % count, i) for i in range(ends)]),
            ],
            axis=dim,
        )
    return cells


def gll_tables():
    points = 8
    gll_nodes = np.array(
        [
            -1.0,
            -0.8717401485096066,
            -0.5917001814331423,
            -0.2092992179024789,
            0.2092992179024789,
            0.5917001814331423,
            0.8717401485096066,
            1.0,
        ]
    )
    previous = np.ones(points)
    current = np.array(gll_nodes)
    for degree in range(1, points - 1):
        previous, current = (
            current,
            ((2 * degree + 1) * gll_nodes * current - degree * previous) / (degree + 1),
        )
    weights = 2.0 / (points * (points - 1) * current**2)
    derivative = np.zeros((points, points))
    for target in range(points):
        for source in range(points):
            if target != source:
                derivative[target, source] = current[target] / (
                    current[source] * (gll_nodes[target] - gll_nodes[source])
                )
    derivative[0, 0] = -points * (points - 1) / 4.0
    derivative[points - 1, points - 1] = points * (points - 1) / 4.0
    return (weights, derivative)


def node_masks(extent, position, devices, periodic):
    local_pos = jnp.arange(extent)
    global_pos = position * extent + local_pos
    first_node = jnp.logical_and(local_pos % 8 == 0, jnp.logical_or(periodic, global_pos > 0))
    last_node = jnp.logical_and(
        local_pos % 8 == 7, jnp.logical_or(periodic, global_pos < devices * extent - 1)
    )
    return (first_node.astype(jnp.float32), last_node.astype(jnp.float32))


def apply_dim(values, matrix, which_dim):
    if which_dim == 0:
        return jnp.einsum("xyz,wx->wyz", values, matrix, precision=lax.Precision.HIGHEST)
    if which_dim == 1:
        return jnp.einsum("xyz,wy->xwz", values, matrix, precision=lax.Precision.HIGHEST)
    return jnp.einsum("xyz,wz->xyw", values, matrix, precision=lax.Precision.HIGHEST)


def combine(padded, which_dim):
    extent = padded.shape[which_dim] - 2
    local_pos = jnp.arange(extent)
    view_shape = [1] * padded.ndim
    view_shape[which_dim] = extent
    first_node = (local_pos % 8 == 0).astype(jnp.float32).reshape(view_shape)
    last_node = (local_pos % 8 == 7).astype(jnp.float32).reshape(view_shape)
    middle = lax.slice_in_dim(padded, 1, extent + 1, axis=which_dim)
    lower_rim = lax.slice_in_dim(padded, 0, extent, axis=which_dim)
    upper_rim = lax.slice_in_dim(padded, 2, extent + 2, axis=which_dim)
    return middle + first_node * lower_rim + last_node * upper_rim


def assemble(values):
    padded = with_halo(values, (("gx", 1),), 1, False)
    values = combine(padded, 1)
    padded = with_halo(values, (("gy", 2),), 1, False)
    values = combine(padded, 2)
    padded = with_halo(values, (("gz", 3),), 1, True)
    return combine(padded, 3)


def per_device(base_flow, adjoint_velocity, penalty):
    weights, derivative = gll_tables()
    extents = penalty.shape
    matrices = [
        jnp.asarray(np.kron(np.eye(extents[which_dim] // 8), derivative), jnp.float32)
        for which_dim in range(3)
    ]
    vectors = [
        jnp.asarray(np.tile(weights, extents[which_dim] // 8), jnp.float32)
        for which_dim in range(3)
    ]
    mass = vectors[0][:, None, None] * vectors[1][None, :, None] * vectors[2][None, None, :]
    positions = (lax.axis_index("gx"), lax.axis_index("gy"), lax.axis_index("gz"))
    devices = (lax.axis_size("gx"), lax.axis_size("gy"), lax.axis_size("gz"))
    counts = []
    for which_dim, periodic in ((0, False), (1, False), (2, True)):
        first_node, last_node = node_masks(
            extents[which_dim], positions[which_dim], devices[which_dim], periodic
        )
        counts.append(1.0 + first_node + last_node)
    mult = counts[0][:, None, None] * counts[1][None, :, None] * counts[2][None, None, :]
    inv_mult = 1.0 / mult
    mass_total = mass * mult
    advection = []
    for comp_i in range(3):
        term = jnp.zeros(extents, jnp.float32)
        for comp_j in range(3):
            term = term - base_flow[comp_j] * apply_dim(
                adjoint_velocity[comp_i], matrices[comp_j], comp_j
            )
            term = term + adjoint_velocity[comp_j] * apply_dim(
                base_flow[comp_j], matrices[comp_i], comp_i
            )
        advection.append(mass * term)
    advc = assemble(jnp.stack(advection)) / mass_total
    divergence = (
        apply_dim(advc[0], matrices[0], 0)
        + apply_dim(advc[1], matrices[1], 1)
        + apply_dim(advc[2], matrices[2], 2)
    )
    rhs = -assemble((mass * divergence)[None])[0]

    def squares(values):
        return lax.psum(jnp.sum(values * values * inv_mult), ("gx", "gy", "gz"))

    pressure = jnp.zeros_like(rhs)
    residual = rhs
    direction = rhs
    norm_now = squares(residual)
    for step in range(ITERS):
        local = penalty * mass * direction
        for operator_which_dim in range(3):
            local = local + apply_dim(
                mass * apply_dim(direction, matrices[operator_which_dim], operator_which_dim),
                matrices[operator_which_dim].T,
                operator_which_dim,
            )
        image = assemble(local[None])[0]
        alpha = norm_now / lax.psum(jnp.sum(direction * image * inv_mult), ("gx", "gy", "gz"))
        pressure = pressure + alpha * direction
        residual = residual - alpha * image
        if step + 1 < ITERS:
            norm_next = squares(residual)
            direction = residual + norm_next / norm_now * direction
            norm_now = norm_next
    gradient = jnp.stack(
        [mass * apply_dim(pressure, matrices[which_dim], which_dim) for which_dim in range(3)]
    )
    projected = advc - assemble(gradient) / mass_total
    return (projected, pressure)


def solution(mesh):
    in_specs = (P(None, "gx", "gy", "gz"), P(None, "gx", "gy", "gz"), P("gx", "gy", "gz"))
    out_specs = (P(None, "gx", "gy", "gz"), P("gx", "gy", "gz"))
    return jax.shard_map(
        per_device, mesh=mesh, in_specs=in_specs, out_specs=out_specs, check_vma=False
    )
```

profile of v0, /device:TPU:1, one launch (start us, length us, event | category | flops | bytes accessed | tf_op | source)
XLA Modules:
  0.0 605.8 jit_solution(2947159668578955404)
XLA Ops:
  11.9 9.6 %collective-permute-start = (f32[3,1,32,128]{3,1,2,0:T(1,128)S(1)}, f32[3,1,32,128]{3,1,2,0:T(1,128)S(1)}, u32[]{:S(2)}, u32[]{:S(2)}) collective-permute-start(f32[3,1,32,128]{3,1,2,0:T(1,128)S(1)} %get-tuple-element.25), channel_id=1, source_target_pairs={{0,32},{32,64},{64,96},{96,128},{128,160},{160,192},{192,224},{1,3... | collective-permute-start | bytes 147464 | tf_op jit(solution)/shard_map/ppermute | solution.py:18
  23.1 7.2 %collective-permute-done.1 = f32[3,1,32,128]{3,1,2,0:T(1,128)S(1)} collective-permute-done((f32[3,1,32,128]{3,1,2,0:T(1,128)S(1)}, f32[3,1,32,128]{3,1,2,0:T(1,128)S(1)}, u32[]{:S(2)}, u32[]{:S(2)}) %collective-permute-start.1) | collective-permute-done | bytes 49184 | tf_op jit(solution)/shard_map/ppermute | solution.py:20
  30.5 3.1 collective-permute-start.2
  34.9 3.1 collective-permute-done.3
  38.4 4.3 collective-permute-start.4
  42.6 5.8 collective-permute-done.4
  48.4 5.8 collective-permute-done.5
  59.7 7.2 %collective-permute-done.7 = f32[1,1,32,128]{3,1,2,0:T(1,128)S(1)} collective-permute-done((f32[1,1,32,128]{3,1,2,0:T(1,128)S(1)}, f32[1,1,32,128]{3,1,2,0:T(1,128)S(1)}, u32[]{:S(2)}, u32[]{:S(2)}) %collective-permute-start.7) | collective-permute-done | bytes 16416 | tf_op jit(solution)/shard_map/ppermute | solution.py:20
  67.0 3.1 collective-permute-start.8
  84.5 6.6 %collective-permute-start.12 = (f32[1,1,32,128]{3,1,2,0:T(1,128)S(1)}, f32[1,1,32,128]{3,1,2,0:T(1,128)S(1)}, u32[]{:S(2)}, u32[]{:S(2)}) collective-permute-start(f32[1,1,32,128]{3,1,2,0:T(1,128)S(1)} %get-tuple-element.49), channel_id=1, source_target_pairs={{0,32},{32,64},{64,96},{96,128},{128,160},{160,192},{192,224},{1,3... | collective-permute-start | bytes 49160 | tf_op jit(solution)/shard_map/ppermute | solution.py:18
  92.4 7.1 %collective-permute-done.13 = f32[1,1,32,128]{3,1,2,0:T(1,128)S(1)} collective-permute-done((f32[1,1,32,128]{3,1,2,0:T(1,128)S(1)}, f32[1,1,32,128]{3,1,2,0:T(1,128)S(1)}, u32[]{:S(2)}, u32[]{:S(2)}) %collective-permute-start.13) | collective-permute-done | bytes 16416 | tf_op jit(solution)/shard_map/ppermute | solution.py:20
  107.0 3.0 collective-permute-start.16
  110.1 4.9 collective-permute-start.17
  116.8 80.1 %all-reduce = (f32[]{:T(128)}, f32[]{:T(128)}) all-reduce(f32[]{:T(128)} %get-tuple-element.5, f32[]{:T(128)} %get-tuple-element.4), channel_id=1, replica_groups=mesh['gx'=8,'gy'=4,'gz'=8] {'gx','gy','gz'}, use_global_device_ids=true, to_apply=%region_1.2 | all-reduce | flops 2 | bytes 16 | tf_op jit(solution)/shard_map/psum | solution.py:144
  198.9 72.6 %psum.44 = f32[]{:T(128)} all-reduce(f32[]{:T(128)} %get-tuple-element.10), channel_id=1, replica_groups=mesh['gx'=8,'gy'=4,'gz'=8] {'gx','gy','gz'}, use_global_device_ids=true, to_apply=%region_5.6 | all-reduce | flops 1 | bytes 8 | tf_op jit(solution)/shard_map/psum | solution.py:144
  274.8 5.2 collective-permute-start.18
  281.4 7.1 %collective-permute-done.19 = f32[1,1,32,128]{3,1,2,0:T(1,128)S(1)} collective-permute-done((f32[1,1,32,128]{3,1,2,0:T(1,128)S(1)}, f32[1,1,32,128]{3,1,2,0:T(1,128)S(1)}, u32[]{:S(2)}, u32[]{:S(2)}) %collective-permute-start.19) | collective-permute-done | bytes 16416 | tf_op jit(solution)/shard_map/ppermute | solution.py:20
  295.1 5.3 collective-permute-start.22
  302.3 3.5 collective-permute-done.23
  306.6 74.8 %psum.45 = f32[]{:T(128)} all-reduce(f32[]{:T(128)} %get-tuple-element.8), channel_id=1, replica_groups=mesh['gx'=8,'gy'=4,'gz'=8] {'gx','gy','gz'}, use_global_device_ids=true, to_apply=%region_7.8 | all-reduce | flops 1 | bytes 8 | tf_op jit(solution)/shard_map/psum | solution.py:159
  383.4 72.6 %psum.46 = f32[]{:T(128)} all-reduce(f32[]{:T(128)} %multiply_reduce_fusion), channel_id=1, replica_groups=mesh['gx'=8,'gy'=4,'gz'=8] {'gx','gy','gz'}, use_global_device_ids=true, to_apply=%region_9.10 | all-reduce | flops 1 | bytes 8 | tf_op jit(solution)/shard_map/psum | solution.py:144
  459.3 4.3 collective-permute-start.24
  465.2 7.0 %collective-permute-done.25 = f32[1,1,32,128]{3,1,2,0:T(1,128)S(1)} collective-permute-done((f32[1,1,32,128]{3,1,2,0:T(1,128)S(1)}, f32[1,1,32,128]{3,1,2,0:T(1,128)S(1)}, u32[]{:S(2)}, u32[]{:S(2)}) %collective-permute-start.25) | collective-permute-done | bytes 16416 | tf_op jit(solution)/shard_map/ppermute | solution.py:20
  479.5 5.4 collective-permute-start.28
  486.8 3.3 collective-permute-done.29
  490.9 74.7 %psum.47 = f32[]{:T(128)} all-reduce(f32[]{:T(128)} %fusion.73), channel_id=1, replica_groups=mesh['gx'=8,'gy'=4,'gz'=8] {'gx','gy','gz'}, use_global_device_ids=true, to_apply=%region_11.12 | all-reduce | flops 1 | bytes 8 | tf_op jit(solution)/shard_map/psum | solution.py:159
  568.4 4.3 collective-permute-start.30
  574.2 7.4 %collective-permute-done.31 = f32[3,1,32,128]{3,1,2,0:T(1,128)S(1)} collective-permute-done((f32[3,1,32,128]{3,1,2,0:T(1,128)S(1)}, f32[3,1,32,128]{3,1,2,0:T(1,128)S(1)}, u32[]{:S(2)}, u32[]{:S(2)}) %collective-permute-start.31) | collective-permute-done | bytes 49184 | tf_op jit(solution)/shard_map/ppermute | solution.py:20
  584.5 3.1 collective-permute-done.33
  588.0 4.8 collective-permute-start.34
  592.8 6.4 %collective-permute-done.34 = f32[3,8,32,1]{3,1,2,0:T(8,128)S(1)} collective-permute-done((f32[3,8,32,1]{3,1,2,0:T(8,128)S(1)}, f32[3,8,32,1]{3,1,2,0:T(8,128)S(1)}, u32[]{:S(2)}, u32[]{:S(2)}) %collective-permute-start.34) | collective-permute-done | bytes 3104 | tf_op jit(solution)/shard_map/ppermute | solution.py:18
  599.2 5.1 collective-permute-done.35
  (167 shorter events, 79.8 us)
Async XLA Ops:
  11.9 11.2 %collective-permute-start = (f32[3,1,32,128]{3,1,2,0:T(1,128)S(1)}, f32[3,1,32,128]{3,1,2,0:T(1,128)S(1)}, u32[]{:S(2)}, u32[]{:S(2)}) collective-permute-start(f32[3,1,32,128]{3,1,2,0:T(1,128)S(1)} %get-tuple-element.25), channel_id=1, source_target_pairs={{0,32},{32,64},{64,96},{96,128},{128,160},{160,192},{192,224},{1,3... | collective-permute-start | bytes 147464 | tf_op jit(solution)/shard_map/ppermute | solution.py:18
  21.5 8.7 %collective-permute-start.1 = (f32[3,1,32,128]{3,1,2,0:T(1,128)S(1)}, f32[3,1,32,128]{3,1,2,0:T(1,128)S(1)}, u32[]{:S(2)}, u32[]{:S(2)}) collective-permute-start(f32[3,1,32,128]{3,1,2,0:T(1,128)S(1)} %get-tuple-element.26), channel_id=1, source_target_pairs={{32,0},{64,32},{96,64},{128,96},{160,128},{192,160},{224,192},{33,... | collective-permute-start | bytes 147464 | tf_op jit(solution)/shard_map/ppermute | solution.py:20
  30.5 4.4 collective-permute-start.2
  33.6 4.4 collective-permute-start.3
  38.4 10.0 %collective-permute-start.4 = (f32[3,8,32,1]{3,1,2,0:T(8,128)S(1)}, f32[3,8,32,1]{3,1,2,0:T(8,128)S(1)}, u32[]{:S(2)}, u32[]{:S(2)}) collective-permute-start(f32[3,8,32,1]{3,1,2,0:T(8,128)S(1)} %get-tuple-element.21), channel_id=1, source_target_pairs={{0,1},{1,2},{2,3},{3,4},{4,5},{5,6},{6,7},{7,0},{8,9},{9,10},{10,1... | collective-permute-start | bytes 9224 | tf_op jit(solution)/shard_map/ppermute | solution.py:18
  42.6 11.6 %collective-permute-start.5 = (f32[3,8,32,1]{3,1,2,0:T(8,128)S(1)}, f32[3,8,32,1]{3,1,2,0:T(8,128)S(1)}, u32[]{:S(2)}, u32[]{:S(2)}) collective-permute-start(f32[3,8,32,1]{3,1,2,0:T(8,128)S(1)} %get-tuple-element.22), channel_id=1, source_target_pairs={{1,0},{2,1},{3,2},{4,3},{5,4},{6,5},{7,6},{0,7},{9,8},{10,9},{11,1... | collective-permute-start | bytes 9224 | tf_op jit(solution)/shard_map/ppermute | solution.py:20
  55.4 4.3 collective-permute-start.6
  58.4 8.5 %collective-permute-start.7 = (f32[1,1,32,128]{3,1,2,0:T(1,128)S(1)}, f32[1,1,32,128]{3,1,2,0:T(1,128)S(1)}, u32[]{:S(2)}, u32[]{:S(2)}) collective-permute-start(f32[1,1,32,128]{3,1,2,0:T(1,128)S(1)} %get-tuple-element.56), channel_id=1, source_target_pairs={{32,0},{64,32},{96,64},{128,96},{160,128},{192,160},{224,192},{33,... | collective-permute-start | bytes 49160 | tf_op jit(solution)/shard_map/ppermute | solution.py:20
  67.0 4.4 collective-permute-start.8
  70.1 4.4 collective-permute-start.9
  74.7 4.8 collective-permute-start.10
  77.4 4.4 collective-permute-start.11
  84.5 7.9 %collective-permute-start.12 = (f32[1,1,32,128]{3,1,2,0:T(1,128)S(1)}, f32[1,1,32,128]{3,1,2,0:T(1,128)S(1)}, u32[]{:S(2)}, u32[]{:S(2)}) collective-permute-start(f32[1,1,32,128]{3,1,2,0:T(1,128)S(1)} %get-tuple-element.49), channel_id=1, source_target_pairs={{0,32},{32,64},{64,96},{96,128},{128,160},{160,192},{192,224},{1,3... | collective-permute-start | bytes 49160 | tf_op jit(solution)/shard_map/ppermute | solution.py:18
  91.1 8.4 %collective-permute-start.13 = (f32[1,1,32,128]{3,1,2,0:T(1,128)S(1)}, f32[1,1,32,128]{3,1,2,0:T(1,128)S(1)}, u32[]{:S(2)}, u32[]{:S(2)}) collective-permute-start(f32[1,1,32,128]{3,1,2,0:T(1,128)S(1)} %get-tuple-element.50), channel_id=1, source_target_pairs={{32,0},{64,32},{96,64},{128,96},{160,128},{192,160},{224,192},{33,... | collective-permute-start | bytes 49160 | tf_op jit(solution)/shard_map/ppermute | solution.py:20
  102.4 4.4 collective-permute-start.15
  107.0 8.7 %collective-permute-start.16 = (f32[1,8,32,1]{3,1,2,0:T(8,128)S(1)}, f32[1,8,32,1]{3,1,2,0:T(8,128)S(1)}, u32[]{:S(2)}, u32[]{:S(2)}) collective-permute-start(f32[1,8,32,1]{3,1,2,0:T(8,128)S(1)} %get-tuple-element.45), channel_id=1, source_target_pairs={{0,1},{1,2},{2,3},{3,4},{4,5},{5,6},{6,7},{7,0},{8,9},{9,10},{10,1... | collective-permute-start | bytes 3080 | tf_op jit(solution)/shard_map/ppermute | solution.py:18
  110.1 5.9 collective-permute-start.17
  274.8 6.5 %collective-permute-start.18 = (f32[1,1,32,128]{3,1,2,0:T(1,128)S(1)}, f32[1,1,32,128]{3,1,2,0:T(1,128)S(1)}, u32[]{:S(2)}, u32[]{:S(2)}) collective-permute-start(f32[1,1,32,128]{3,1,2,0:T(1,128)S(1)} %get-tuple-element.43), channel_id=1, source_target_pairs={{0,32},{32,64},{64,96},{96,128},{128,160},{160,192},{192,224},{1,3... | collective-permute-start | bytes 49160 | tf_op jit(solution)/shard_map/ppermute | solution.py:18
  280.1 8.4 %collective-permute-start.19 = (f32[1,1,32,128]{3,1,2,0:T(1,128)S(1)}, f32[1,1,32,128]{3,1,2,0:T(1,128)S(1)}, u32[]{:S(2)}, u32[]{:S(2)}) collective-permute-start(f32[1,1,32,128]{3,1,2,0:T(1,128)S(1)} %get-tuple-element.44), channel_id=1, source_target_pairs={{32,0},{64,32},{96,64},{128,96},{160,128},{192,160},{224,192},{33,... | collective-permute-start | bytes 49160 | tf_op jit(solution)/shard_map/ppermute | solution.py:20
  290.5 4.4 collective-permute-start.21
  295.1 7.2 %collective-permute-start.22 = (f32[1,8,32,1]{3,1,2,0:T(8,128)S(1)}, f32[1,8,32,1]{3,1,2,0:T(8,128)S(1)}, u32[]{:S(2)}, u32[]{:S(2)}) collective-permute-start(f32[1,8,32,1]{3,1,2,0:T(8,128)S(1)} %get-tuple-element.39), channel_id=1, source_target_pairs={{0,1},{1,2},{2,3},{3,4},{4,5},{5,6},{6,7},{7,0},{8,9},{9,10},{10,1... | collective-permute-start | bytes 3080 | tf_op jit(solution)/shard_map/ppermute | solution.py:18
  300.4 5.4 collective-permute-start.23
  459.3 5.9 collective-permute-start.24
  463.6 8.5 %collective-permute-start.25 = (f32[1,1,32,128]{3,1,2,0:T(1,128)S(1)}, f32[1,1,32,128]{3,1,2,0:T(1,128)S(1)}, u32[]{:S(2)}, u32[]{:S(2)}) collective-permute-start(f32[1,1,32,128]{3,1,2,0:T(1,128)S(1)} %get-tuple-element.38), channel_id=1, source_target_pairs={{32,0},{64,32},{96,64},{128,96},{160,128},{192,160},{224,192},{33,... | collective-permute-start | bytes 49160 | tf_op jit(solution)/shard_map/ppermute | solution.py:20
  474.9 4.4 collective-permute-start.27
  479.5 7.3 %collective-permute-start.28 = (f32[1,8,32,1]{3,1,2,0:T(8,128)S(1)}, f32[1,8,32,1]{3,1,2,0:T(8,128)S(1)}, u32[]{:S(2)}, u32[]{:S(2)}) collective-permute-start(f32[1,8,32,1]{3,1,2,0:T(8,128)S(1)} %get-tuple-element.33), channel_id=1, source_target_pairs={{0,1},{1,2},{2,3},{3,4},{4,5},{5,6},{6,7},{7,0},{8,9},{9,10},{10,1... | collective-permute-start | bytes 3080 | tf_op jit(solution)/shard_map/ppermute | solution.py:18
  484.9 5.2 collective-permute-start.29
  568.4 5.7 collective-permute-start.30
  572.8 8.8 %collective-permute-start.31 = (f32[3,1,32,128]{3,1,2,0:T(1,128)S(1)}, f32[3,1,32,128]{3,1,2,0:T(1,128)S(1)}, u32[]{:S(2)}, u32[]{:S(2)}) collective-permute-start(f32[3,1,32,128]{3,1,2,0:T(1,128)S(1)} %get-tuple-element.20), channel_id=1, source_target_pairs={{32,0},{64,32},{96,64},{128,96},{160,128},{192,160},{224,192},{33,... | collective-permute-start | bytes 147464 | tf_op jit(solution)/shard_map/ppermute | solution.py:20
  583.2 4.4 collective-permute-start.33
  588.0 11.2 %collective-permute-start.34 = (f32[3,8,32,1]{3,1,2,0:T(8,128)S(1)}, f32[3,8,32,1]{3,1,2,0:T(8,128)S(1)}, u32[]{:S(2)}, u32[]{:S(2)}) collective-permute-start(f32[3,8,32,1]{3,1,2,0:T(8,128)S(1)} %get-tuple-element.15), channel_id=1, source_target_pairs={{0,1},{1,2},{2,3},{3,4},{4,5},{5,6},{6,7},{7,0},{8,9},{9,10},{10,1... | collective-permute-start | bytes 9224 | tf_op jit(solution)/shard_map/ppermute | solution.py:18
  592.8 11.5 %collective-permute-start.35 = (f32[3,8,32,1]{3,1,2,0:T(8,128)S(1)}, f32[3,8,32,1]{3,1,2,0:T(8,128)S(1)}, u32[]{:S(2)}, u32[]{:S(2)}) collective-permute-start(f32[3,8,32,1]{3,1,2,0:T(8,128)S(1)} %get-tuple-element.16), channel_id=1, source_target_pairs={{1,0},{2,1},{3,2},{4,3},{5,4},{6,5},{7,6},{0,7},{9,8},{10,9},{11,1... | collective-permute-start | bytes 9224 | tf_op jit(solution)/shard_map/ppermute | solution.py:20
  (14 other events, 26.2 us)
where the time goes:
time: 608 us; the launch traced here: 606 us
  blocking collectives  375 us (62%)
  waiting for transfers between devices  98.9 us (16%)
  starting transfers between devices  95.7 us (16%)
  matrix products  14.9 us (2%)
  between operations  8.36 us (1%)
  other arithmetic  7.5 us (1%)
    psum x3, blocking collectives, squares(): return lax.psum(jnp.sum(values * values * inv_mult), ('gx', 'gy', 'gz'))  225 us
    psum x2, blocking collectives, per_device(): lax.psum(jnp.sum(direction * image * inv_mult), ('gx', 'gy', 'gz'))  149 us
    ppermute x18, waiting for transfers between devices, with_halo(): lax.ppermute(head, axis, [((i + 1) % count, i) for i in range(ends)])  81.4 us
    ppermute x18, starting transfers between devices, with_halo(): lax.ppermute(tail, axis, [(i, (i + 1) % count) for i in range(ends)])  73.6 us
    ppermute x18, starting transfers between devices, with_halo(): lax.ppermute(head, axis, [((i + 1) % count, i) for i in range(ends)])  22.2 us
    ppermute x18, waiting for transfers between devices, with_halo(): lax.ppermute(tail, axis, [(i, (i + 1) % count) for i in range(ends)])  17.5 us
  transfers between devices with their start and end apart: 36, of which 25 were waited for; matrix products, arithmetic and copies ran while one was open for 0% of the time, Pallas kernels for 0%

commit v1 on v0

v1 whole, which is shorter than its diff:
```python
import functools

import jax
import jax.numpy as jnp
import numpy as np
from jax import lax
from jax.experimental import pallas as pl
from jax.experimental.pallas import tpu as pltpu
from jax.sharding import PartitionSpec as P

MESH = pl.DeviceIdType.MESH
F32 = jnp.float32
HI = lax.Precision.HIGHEST
N = 8
NX, NY, NZ = 8, 32, 128
ROWS = NX * NY
GX, GY, GZ = 8, 4, 8


def gll_tables():
    points = 8
    nodes = np.array(
        [
            -1.0,
            -0.8717401485096066,
            -0.5917001814331423,
            -0.2092992179024789,
            0.2092992179024789,
            0.5917001814331423,
            0.8717401485096066,
            1.0,
        ]
    )
    previous = np.ones(points)
    current = np.array(nodes)
    for degree in range(1, points - 1):
        previous, current = (
            current,
            ((2 * degree + 1) * nodes * current - degree * previous) / (degree + 1),
        )
    weights = 2.0 / (points * (points - 1) * current**2)
    derivative = np.zeros((points, points))
    for target in range(points):
        for source in range(points):
            if target != source:
                derivative[target, source] = current[target] / (
                    current[source] * (nodes[target] - nodes[source])
                )
    derivative[0, 0] = -points * (points - 1) / 4.0
    derivative[points - 1, points - 1] = points * (points - 1) / 4.0
    return weights, derivative


W, D = gll_tables()
L = (D.T * W) @ D / W[:, None]


def average(extent):
    m = np.eye(extent)
    for k in range(8, extent, 8):
        m[k - 1, k - 1] = m[k, k] = m[k - 1, k] = m[k, k - 1] = 0.5
    return m


def along(matrix, extent):
    return np.kron(np.eye(extent // 8), matrix)


def over_y(matrix):
    return np.kron(np.eye(NX), matrix)


def face_rows_y(matrix):
    rows = np.zeros((16, ROWS))
    full = along(matrix, NY)
    for x in range(NX):
        rows[x, x * NY : (x + 1) * NY] = full[0]
        rows[8 + x, x * NY : (x + 1) * NY] = full[NY - 1]
    return rows


def face_rows_z(matrix):
    rows = np.zeros((16, NZ))
    full = along(matrix, NZ)
    rows[0] = full[0]
    rows[8] = full[NZ - 1]
    return rows


def tables():
    ay, az = average(NY), average(NZ)
    y_first = over_y(along(D, NY))
    y_second = np.concatenate(
        [
            over_y(ay),
            over_y(ay @ along(D, NY)),
            face_rows_y(D),
            over_y(ay @ along(L, NY)),
            face_rows_y(L),
        ]
    )
    local = np.arange(8)
    edge = np.where((local == 0) | (local == 7), 2.0, 1.0)
    wyz = W[:, None] * np.tile(W, 16)[None, :]
    myz = edge[:, None] * np.tile(edge, 16)[None, :]
    picks = np.zeros((16, NZ))
    picks[0, 0] = 1.0
    picks[8, NZ - 1] = 1.0
    z_all = np.concatenate(
        [
            along(D, NZ).T,
            az.T,
            (az @ along(D, NZ)).T,
            (az @ along(L, NZ)).T,
            face_rows_z(D),
            face_rows_z(L),
            picks,
            wyz,
            wyz * myz,
            1.0 / myz,
        ]
    )
    return [np.asarray(t, np.float32) for t in (y_first, y_second, z_all)]


Y_AVG, Y_DA, Y_DF, Y_LA, Y_LF = 0, 256, 512, 528, 784
Z_D, Z_AVG, Z_DA, Z_LA, Z_DF, Z_LF, Z_PICK, Z_W, Z_WM, Z_IM = (
    0,
    128,
    256,
    384,
    512,
    528,
    544,
    560,
    568,
    576,
)


def dot(a, b):
    return lax.dot_general(
        a, b, (((1,), (0,)), ((), ())), precision=HI, preferred_element_type=F32
    )


def dot_nt(a, b):
    return lax.dot_general(
        a, b, (((1,), (1,)), ((), ())), precision=HI, preferred_element_type=F32
    )


def dot_tn(a, b):
    return lax.dot_general(
        a, b, (((0,), (0,)), ((), ())), precision=HI, preferred_element_type=F32
    )


def flat(value):
    return value.reshape(ROWS, NZ)


def cube(value):
    return value.reshape(NX, NY, NZ)


def line(matrix_row, tiles):
    total = None
    for coefficient, tile in zip(matrix_row, tiles):
        part = tile * float(np.float32(coefficient))
        total = part if total is None else total + part
    return total


def kernel(
    base,
    adj,
    pen,
    yfirst,
    ysecond,
    zall,
    projected,
    pressure,
    bs,
    us,
    ps,
    y1,
    y2,
    zt,
    raw,
    za,
    ya,
    adv,
    pav,
    vec,
    tt,
    grad,
    wm,
    fz1,
    rz1,
    fy1,
    ry1,
    rx1,
    rxp,
    fx,
    rx,
    fy,
    ry,
    fz,
    rz,
    gfx,
    grx,
    gfy,
    gry,
    gfz,
    grz,
    mom,
    red1,
    part,
    red2,
    load_sem,
    send_sem,
    recv_sem,
    red_send,
    red_recv,
    out_sem,
):
    px = lax.axis_index("gx")
    py = lax.axis_index("gy")
    pz = lax.axis_index("gz")

    def at_x(offset):
        return (lax.rem(px + offset + GX, GX), py, pz)

    def at_y(offset):
        return (px, lax.rem(py + offset + GY, GY), pz)

    def at_z(offset):
        return (px, py, lax.rem(pz + offset + GZ, GZ))

    row = px // 2
    half = lax.rem(px, 2)
    index1 = half * 8 + pz
    index2 = row * 4 + py

    def group1(k):
        i = lax.rem(index1 + k, 16)
        return (row * 2 + i // 8, py, lax.rem(i, 8))

    def group2(k):
        i = lax.rem(index2 + k, 16)
        return ((i // 4) * 2 + half, lax.rem(i, 4), pz)

    loads = [
        pltpu.make_async_copy(adj, us, load_sem.at[0]),
        pltpu.make_async_copy(base, bs, load_sem.at[1]),
        pltpu.make_async_copy(yfirst, y1, load_sem.at[2]),
        pltpu.make_async_copy(zall, zt, load_sem.at[3]),
        pltpu.make_async_copy(pen, ps, load_sem.at[4]),
        pltpu.make_async_copy(ysecond, y2, load_sem.at[5]),
    ]
    for copy in loads:
        copy.start()

    barrier = pltpu.get_barrier_semaphore()
    for k in range(1, 16):
        pl.semaphore_signal(barrier, inc=1, device_id=group1(k), device_id_type=MESH)
        pl.semaphore_signal(barrier, inc=1, device_id=group2(k), device_id_type=MESH)
    for k in (-1, 1):
        pl.semaphore_signal(barrier, inc=1, device_id=at_x(k), device_id_type=MESH)

    hx = (jnp.where(px > 0, 0.5, 0.0), jnp.where(px < GX - 1, 0.5, 0.0))
    hy = (jnp.where(py > 0, 0.5, 0.0), jnp.where(py < GY - 1, 0.5, 0.0))
    sub = lax.broadcasted_iota(jnp.int32, (8, NZ), 0)
    first = jnp.where(sub == 0, 1.0, 0.0)
    last = jnp.where(sub == 7, 1.0, 0.0)

    pending = []
    counter = [0]

    def send(src, dst, device):
        k = counter[0]
        counter[0] += 1
        copy = pltpu.make_async_remote_copy(
            src_ref=src,
            dst_ref=dst,
            send_sem=send_sem.at[k],
            recv_sem=recv_sem.at[k],
            device_id=device,
            device_id_type=MESH,
        )
        copy.start()
        pending.append(copy)
        return copy

    for copy in loads[:4]:
        copy.wait()

    def tiles(ref, yt):
        return [ref[x, pl.ds(8 * yt, 8), :] for x in range(NX)]

    dz_table = zt[pl.ds(Z_D, 128), :]
    for i in range(3):
        ui = us.at[i]
        dy = cube(dot(y1[...], flat(ui[...])))
        dz = cube(dot(flat(ui[...]), dz_table))
        raw[i] = -(bs[1] * dy + bs[2] * dz)
    for j in range(3):
        uj = bs.at[j]
        raw[1] += us[j] * cube(dot(y1[...], flat(uj[...])))
        raw[2] += us[j] * cube(dot(flat(uj[...]), dz_table))
    for yt in range(4):
        rows = pl.ds(8 * yt, 8)
        for i in range(3):
            src = tiles(us.at[i], yt)
            for x in range(NX):
                raw[i, x, rows, :] -= bs[0, x, rows, :] * line(D[x], src)
        for j in range(3):
            src = tiles(bs.at[j], yt)
            for x in range(NX):
                raw[0, x, rows, :] += us[j, x, rows, :] * line(D[x], src)
    loads[4].wait()
    raw[3] = ps[...]

    avg_z = zt[pl.ds(Z_AVG, 128), :]
    pick = zt[pl.ds(Z_PICK, 16), :]
    faces = None
    for i in range(4):
        own = dot_nt(pick, flat(raw[i]))
        if i == 0:
            faces = own
        else:
            faces = faces + pltpu.roll(own, i, 0)
    fz1[...] = faces
    pl.semaphore_wait(barrier, 32)
    copies = [
        send(fz1.at[pl.ds(0, 8)], rz1.at[pl.ds(8, 8)], at_z(-1)),
        send(fz1.at[pl.ds(8, 8)], rz1.at[pl.ds(0, 8)], at_z(1)),
    ]
    for i in range(4):
        za[i] = cube(dot(flat(raw[i]), avg_z))
    for copy in copies:
        copy.wait_recv()
    delta = 0.5 * (rz1[...] - fz1[...])
    for i in range(4):
        pick_i = pick if i == 0 else pltpu.roll(pick, i, 0)
        za[i] += cube(dot_tn(delta, pick_i))
    loads[5].wait()
    for i in range(4):
        for x in range(NX):
            fy1[0, i, pl.ds(x, 1), :] = za[i, x, pl.ds(0, 1), :]
            fy1[1, i, pl.ds(x, 1), :] = za[i, x, pl.ds(NY - 1, 1), :]
    copies = [
        send(fy1.at[0], ry1.at[1], at_y(-1)),
        send(fy1.at[1], ry1.at[0], at_y(1)),
    ]
    avg_y = y2[pl.ds(Y_AVG, 256), :]
    for i in range(4):
        ya[i] = cube(dot(avg_y, flat(za[i])))
    for copy in copies:
        copy.wait_recv()

    def add_y(target, low, high):
        for x in range(NX):
            target[x, pl.ds(0, 8), :] += first * low[x : x + 1, :]
            target[x, pl.ds(NY - 8, 8), :] += last * high[x : x + 1, :]

    for i in range(4):
        add_y(
            ya.at[i],
            hy[0] * (ry1[0, i] - fy1[0, i]),
            hy[1] * (ry1[1, i] - fy1[1, i]),
        )
    copies = [
        send(ya.at[pl.ds(0, 3), 0], rx1.at[1], at_x(-1)),
        send(ya.at[pl.ds(0, 3), NX - 1], rx1.at[0], at_x(1)),
    ]
    copies_p = [
        send(ya.at[3, 0], rxp.at[1], at_x(-1)),
        send(ya.at[3, NX - 1], rxp.at[0], at_x(1)),
    ]

    w_tile = zt[pl.ds(Z_W, 8), :]
    wm_tile = zt[pl.ds(Z_WM, 8), :]
    im_tile = zt[pl.ds(Z_IM, 8), :]
    fix_low = 1.0 - first * (0.5 - hy[0])
    fix_high = 1.0 - last * (0.5 - hy[1])
    inv_low = 1.0 + first * (1.0 - 2.0 * hy[0])
    inv_high = 1.0 + last * (1.0 - 2.0 * hy[1])
    wm_y = [wm_tile * fix_low, wm_tile, wm_tile, wm_tile * fix_high]
    im_y = [im_tile * inv_low, im_tile, im_tile, im_tile * inv_high]
    scale_x = [float(w) for w in W]
    mult_x = [1.0 + 2.0 * hx[0]] + [1.0] * 6 + [1.0 + 2.0 * hx[1]]
    inv_x = [1.0 - hx[0]] + [1.0] * 6 + [1.0 - hx[1]]
    for yt in range(4):
        for x in range(NX):
            wm[x, pl.ds(8 * yt, 8), :] = wm_y[yt] * (mult_x[x] * scale_x[x])

    for i in range(3):
        for x in range(1, NX - 1):
            adv[i, x] = ya[i, x]
    for copy in copies:
        copy.wait_recv()
    for i in range(3):
        adv[i, 0] = ya[i, 0] + hx[0] * (rx1[0, i] - ya[i, 0])
        adv[i, NX - 1] = ya[i, NX - 1] + hx[1] * (rx1[1, i] - ya[i, NX - 1])

    def local(vx, vy, vz, mx, ymat, zmat, with_mass):
        yz = cube(dot(y2[pl.ds(ymat, 256), :], flat(vy[...]))) + cube(
            dot(flat(vz[...]), zt[pl.ds(zmat, 128), :])
        )
        if with_mass:
            yz = yz + pav[...] * vx[...]
        tt[...] = yz
        for yt in range(4):
            src = tiles(vx, yt)
            for x in range(NX):
                tt[x, pl.ds(8 * yt, 8), :] += line(mx[x], src)

    def x_faces(source, mx, low, high):
        for yt in range(4):
            src = tiles(source, yt)
            low[pl.ds(8 * yt, 8), :] = line(mx[0], src)
            high[pl.ds(8 * yt, 8), :] = line(mx[NX - 1], src)

    def add_z(target, delta_z):
        target[...] += cube(dot_tn(delta_z, pick))

    def phase(k, vx, vy, vz, mx, ymat, yface, zmat, zface, with_mass, sign):
        x_faces(vx, mx, fx.at[k, 0], fx.at[k, 1])
        sx = [
            send(fx.at[k, 0], rx.at[k, 1], at_x(-1)),
            send(fx.at[k, 1], rx.at[k, 0], at_x(1)),
        ]
        fz[k] = dot_nt(zt[pl.ds(zface, 16), :], flat(vz[...]))
        sz = [
            send(fz.at[k, pl.ds(0, 8)], rz.at[k, pl.ds(8, 8)], at_z(-1)),
            send(fz.at[k, pl.ds(8, 8)], rz.at[k, pl.ds(0, 8)], at_z(1)),
        ]
        fy[k] = dot(y2[pl.ds(yface, 16), :], flat(vy[...]))
        sy = [
            send(fy.at[k, pl.ds(0, 8)], ry.at[k, pl.ds(8, 8)], at_y(-1)),
            send(fy.at[k, pl.ds(8, 8)], ry.at[k, pl.ds(0, 8)], at_y(1)),
        ]
        if with_mass and k == 1:
            finish_penalty()
        local(vx, vy, vz, mx, ymat, zmat, with_mass)
        for copy in sy:
            copy.wait_recv()
        add_y(
            tt,
            hy[0] * (ry[k, pl.ds(0, 8), :] - fy[k, pl.ds(0, 8), :]),
            hy[1] * (ry[k, pl.ds(8, 8), :] - fy[k, pl.ds(8, 8), :]),
        )
        for copy in sz:
            copy.wait_recv()
        add_z(tt, 0.5 * (rz[k] - fz[k]))
        out = vec.at[k]
        for x in range(1, NX - 1):
            out[x] = tt[x] * (sign * wm[x])
        for copy in sx:
            copy.wait_recv()
        out[0] = (tt[0] + hx[0] * (rx[k, 0] - fx[k, 0])) * (sign * wm[0])
        out[NX - 1] = (tt[NX - 1] + hx[1] * (rx[k, 1] - fx[k, 1])) * (sign * wm[NX - 1])

    def finish_penalty():
        for x in range(1, NX - 1):
            pav[x] = ya[3, x]
        for copy in copies_p:
            copy.wait_recv()
        pav[0] = ya[3, 0] + hx[0] * (rxp[0] - ya[3, 0])
        pav[NX - 1] = ya[3, NX - 1] + hx[1] * (rxp[1] - ya[3, NX - 1])

    phase(0, adv.at[0], adv.at[1], adv.at[2], D, Y_DA, Y_DF, Z_DA, Z_DF, False, -1.0)
    for k in (1, 2):
        v = vec.at[k - 1]
        phase(k, v, v, v, L, Y_LA, Y_LF, Z_LA, Z_LF, True, 1.0)

    def inner(a, b):
        total = None
        for yt in range(4):
            rows = pl.ds(8 * yt, 8)
            s = None
            for x in range(NX):
                p = a[x, rows, :] * b[x, rows, :]
                if x in (0, NX - 1):
                    p = p * inv_x[x]
                s = p if s is None else s + p
            s = s * im_y[yt]
            total = s if total is None else total + s
        return jnp.sum(total, axis=0, keepdims=True)

    v0, v1, v2 = vec.at[0], vec.at[1], vec.at[2]
    local(v2, v2, v2, L, Y_LA, Z_LA, True)
    total = None
    for yt in range(4):
        rows = pl.ds(8 * yt, 8)
        s = None
        for x in range(NX):
            p = v2[x, rows, :] * tt[x, rows, :] * scale_x[x]
            s = p if s is None else s + p
        total = s if total is None else total + s
    mom[pl.ds(5, 1), :] = jnp.sum(total * w_tile, axis=0, keepdims=True)
    mom[pl.ds(0, 1), :] = inner(v0, v0)
    mom[pl.ds(1, 1), :] = inner(v0, v1)
    mom[pl.ds(2, 1), :] = inner(v1, v1)
    mom[pl.ds(3, 1), :] = inner(v1, v2)
    mom[pl.ds(4, 1), :] = inner(v2, v2)
    mom[pl.ds(6, 2), :] = jnp.zeros((2, NZ), F32)

    def spread(source, slots, own, group, which):
        slots[own] = source[...]
        for k in range(1, 16):
            copy = pltpu.make_async_remote_copy(
                src_ref=source,
                dst_ref=slots.at[own],
                send_sem=red_send.at[which, k],
                recv_sem=red_recv.at[which],
                device_id=group(k),
                device_id_type=MESH,
            )
            copy.start()
            pending.append(copy)

    def gather(slots, which):
        view = slots.at[pl.ds(0, 15)]
        pltpu.make_async_copy(view, view, red_recv.at[which]).wait()
        total = slots[0]
        for k in range(1, 16):
            total = total + slots[k]
        return total

    spread(mom, red1, index1, group1, 0)

    zpick = zt[pl.ds(Z_DF, 16), :]
    for k in range(3):
        v = vec.at[k]
        x_faces(v, D, gfx.at[0, k], gfx.at[1, k])
        gfy[:, k] = dot(y2[pl.ds(Y_DF, 16), :], flat(v[...])).reshape(2, 8, NZ)
    faces = None
    for k in range(3):
        own = dot_nt(zpick, flat(vec[k]))
        faces = own if k == 0 else faces + pltpu.roll(own, k, 0)
    gfz[...] = faces
    gsend = [
        send(gfx.at[0], grx.at[1], at_x(-1)),
        send(gfx.at[1], grx.at[0], at_x(1)),
        send(gfz.at[pl.ds(0, 8)], grz.at[pl.ds(8, 8)], at_z(-1)),
        send(gfz.at[pl.ds(8, 8)], grz.at[pl.ds(0, 8)], at_z(1)),
        send(gfy.at[0], gry.at[1], at_y(-1)),
        send(gfy.at[1], gry.at[0], at_y(1)),
    ]
    part[...] = gather(red1, 0)
    spread(part, red2, index2, group2, 1)
    for k in range(3):
        v = vec.at[k]
        grad[k, 1] = cube(dot(y2[pl.ds(Y_DA, 256), :], flat(v[...])))
        grad[k, 2] = cube(dot(flat(v[...]), zt[pl.ds(Z_DA, 128), :]))
        for yt in range(4):
            src = tiles(v, yt)
            for x in range(NX):
                grad[k, 0, x, pl.ds(8 * yt, 8), :] = line(D[x], src)
    for copy in gsend:
        copy.wait_recv()
    delta_z = 0.5 * (grz[...] - gfz[...])
    for k in range(3):
        grad[k, 0, 0] += hx[0] * (grx[0, k] - gfx[0, k])
        grad[k, 0, NX - 1] += hx[1] * (grx[1, k] - gfx[1, k])
        add_y(
            grad.at[k, 1],
            hy[0] * (gry[0, k] - gfy[0, k]),
            hy[1] * (gry[1, k] - gfy[1, k]),
        )
        pick_k = pick if k == 0 else pltpu.roll(pick, k, 0)
        grad[k, 2] += cube(dot_tn(delta_z, pick_k))

    sums = jnp.sum(gather(red2, 1), axis=1, keepdims=True)
    m = [jnp.broadcast_to(sums[k : k + 1, :], (8, NZ)) for k in range(6)]
    s0, s1, s2 = lax.rsqrt(m[1]), lax.rsqrt(m[3]), lax.rsqrt(m[5])
    h01 = m[2] * s0 * s1
    h02 = m[3] * s0 * s2
    h12 = m[4] * s1 * s2
    h00, h11, h22 = m[1] * s0 * s0, m[3] * s1 * s1, m[5] * s2 * s2
    g0, g1, g2 = m[0] * s0, m[1] * s1, m[2] * s2
    l10 = h01 / h00
    l20 = h02 / h00
    d1 = h11 - l10 * h01
    e1 = h12 - l20 * h01
    l21 = e1 / d1
    d2 = h22 - l20 * h02 - l21 * e1
    y0 = g0
    y1_ = g1 - l10 * y0
    y2_ = g2 - l20 * y0 - l21 * y1_
    c2 = y2_ / d2
    c1 = y1_ / d1 - l21 * c2
    c0 = y0 / h00 - l10 * c1 - l20 * c2
    c0, c1, c2 = c0 * s0, c1 * s1, c2 * s2

    for yt in range(4):
        rows = pl.ds(8 * yt, 8)
        for x in range(NX):
            tt[x, rows, :] = (
                c0 * v0[x, rows, :] + c1 * v1[x, rows, :] + c2 * v2[x, rows, :]
            )
            for i in range(3):
                raw[i, x, rows, :] = adv[i, x, rows, :] - (
                    c0 * grad[0, i, x, rows, :]
                    + c1 * grad[1, i, x, rows, :]
                    + c2 * grad[2, i, x, rows, :]
                )
    outs = [
        pltpu.make_async_copy(raw.at[pl.ds(0, 3)], projected, out_sem.at[0]),
        pltpu.make_async_copy(tt, pressure, out_sem.at[1]),
    ]
    for copy in outs:
        copy.start()
    for copy in pending:
        copy.wait_send()
    for copy in outs:
        copy.wait()


def per_device(base_flow, adjoint_velocity, penalty):
    field = (NX, NY, NZ)
    v = lambda *shape: pltpu.VMEM(shape, F32)
    consts = [jnp.asarray(t) for t in tables()]
    any_spec = pl.BlockSpec(memory_space=pltpu.HBM)
    sends = 30
    return pl.pallas_call(
        kernel,
        out_shape=(
            jax.ShapeDtypeStruct((3,) + field, F32),
            jax.ShapeDtypeStruct(field, F32),
        ),
        in_specs=[any_spec] * 6,
        out_specs=(any_spec, any_spec),
        scratch_shapes=[
            v(3, *field),
            v(3, *field),
            v(*field),
            v(*consts[0].shape),
            v(*consts[1].shape),
            v(*consts[2].shape),
            v(4, *field),
            v(4, *field),
            v(4, *field),
            v(3, *field),
            v(*field),
            v(3, *field),
            v(*field),
            v(3, 3, *field),
            v(*field),
            v(16, ROWS),
            v(16, ROWS),
            v(2, 4, 8, NZ),
            v(2, 4, 8, NZ),
            v(2, 3, NY, NZ),
            v(2, NY, NZ),
            v(3, 2, NY, NZ),
            v(3, 2, NY, NZ),
            v(3, 16, NZ),
            v(3, 16, NZ),
            v(3, 16, ROWS),
            v(3, 16, ROWS),
            v(2, 3, NY, NZ),
            v(2, 3, NY, NZ),
            v(2, 3, 8, NZ),
            v(2, 3, 8, NZ),
            v(16, ROWS),
            v(16, ROWS),
            v(8, NZ),
            v(16, 8, NZ),
            v(8, NZ),
            v(16, 8, NZ),
            pltpu.SemaphoreType.DMA((6,)),
            pltpu.SemaphoreType.DMA((sends + 10,)),
            pltpu.SemaphoreType.DMA((sends + 10,)),
            pltpu.SemaphoreType.DMA((2, 16)),
            pltpu.SemaphoreType.DMA((2,)),
            pltpu.SemaphoreType.DMA((2,)),
        ],
        compiler_params=pltpu.CompilerParams(
            collective_id=0, has_side_effects=True, vmem_limit_bytes=63 * 1024 * 1024
        ),
        name="adjoint",
    )(base_flow, adjoint_velocity, penalty, *consts)


def solution(mesh):
    spec3 = P(None, "gx", "gy", "gz")
    spec1 = P("gx", "gy", "gz")
    return jax.shard_map(
        per_device,
        mesh=mesh,
        in_specs=(spec3, spec3, spec1),
        out_specs=(spec3, spec1),
        check_vma=False,
    )
```

time: 608 us -> 59.4 us (0.10)
  blocking collectives: 375 us -> 0 us
  waiting for transfers between devices: 98.9 us -> 0 us
  starting transfers between devices: 95.7 us -> 0 us
  Pallas kernels: 0 us -> 56.1 us
  matrix products: 14.9 us -> 0 us
  between operations: 8.36 us -> 0.65 us
  other arithmetic: 7.5 us -> 0 us
    psum x5 -> x0, blocking collectives: 375 us -> none  [the longest x3 225 us: squares(): return lax.psum(jnp.sum(values * values * inv_mult), ('gx', 'gy', 'gz'))]
    ppermute x36 -> x0, waiting for transfers between devices: 98.9 us -> none  [the longest x18 81.4 us: with_halo(): lax.ppermute(head, axis, [((i + 1) % count, i) for i in range(ends)])]
    ppermute x36 -> x0, starting transfers between devices: 95.7 us -> none  [the longest x18 73.6 us: with_halo(): lax.ppermute(tail, axis, [(i, (i + 1) % count) for i in range(ends)])]
    pallas_call x0 -> x1, Pallas kernels: none -> 56.1 us  [per_device(): pl.pallas_call(kernel, out_shape=(jax.ShapeDtypeStruct((3,) + field, F32)...]
    dot_general x42 -> x0, matrix products: 14.9 us -> none  [the longest x14 5.58 us: apply_dim(): jnp.einsum('xyz,wy->xwz', values, matrix, precision=lax.Precision.HIGHEST)]
  transfers between devices with their start and end apart: 36 -> 0, of which waited for: 25 -> 0; matrix products, arithmetic and copies ran while one was open for 0% -> 0% of each run, Pallas kernels for 0% -> 0%
where the time goes in v1:
time: 59.4 us; the launch traced here: 59.2 us
  Pallas kernels  56.1 us (94%)
  local copies, waits for them, and re-layouts  2.46 us (4%)
  between operations  0.65 us (1%)
    pallas_call x1, Pallas kernels, per_device(): pl.pallas_call(kernel, out_shape=(jax.ShapeDtypeStruct((3,) + field, F32)...  56.1 us
    unnamed x4, local copies, waits for them, and re-layouts  2.46 us

profile of v1, /device:TPU:1, one launch (start us, length us, event | category | flops | bytes accessed | tf_op | source)
XLA Modules:
  0.0 59.2 jit_solution(15287960362194021965)
XLA Ops:
  0.6 56.1 %adjoint.1 = (f32[3,8,32,128]{3,2,1,0:T(8,128)}, f32[8,32,128]{2,1,0:T(8,128)}) custom-call(f32[3,8,32,128]{3,2,1,0:T(8,128)} %base.1, f32[3,8,32,128]{3,2,1,0:T(8,128)} %adj.1, f32[8,32,128]{2,1,0:T(8,128)} %pen.1, f32[256,256]{1,0:T(8,128)} %constant.6.clone.yfirst, f32[800,256]{1,0:T(8,128)} %constant.7.clone.ysecond, f32[584,128]{1,0:T(8,128)} %constant.8.clone.zall), custom_call_target="tpu_custom_call" | custom-call | tf_op jit(solution)/shard_map/adjoint/pallas_call | solution.py:629
  56.8 0.0 copy-start
  56.8 1.8 %copy.10 = f32[3,8,32,128]{3,2,1,0:T(8,128)} copy(f32[3,8,32,128]{3,2,1,0:T(8,128)} %get-tuple-element.4) | data formatting | bytes 786432
  58.6 0.0 copy-done
  58.6 0.7 %copy.11 = f32[8,32,128]{2,1,0:T(8,128)} copy(f32[8,32,128]{2,1,0:T(8,128)S(1)} %copy-done) | data formatting | bytes 262144
Async XLA Ops:
  56.8 1.8 %copy-start = (f32[8,32,128]{2,1,0:T(8,128)S(1)}, f32[8,32,128]{2,1,0:T(8,128)}, u32[]{:S(2)}) copy-start(f32[8,32,128]{2,1,0:T(8,128)} %get-tuple-element.5) | copy-start | bytes 393220

commit v2 on v1

--- a/solution.py
+++ b/solution.py
@@ -2,6 +2,7 @@
 
 import jax
 import jax.numpy as jnp
+import ml_dtypes
 import numpy as np
 from jax import lax
 from jax.experimental import pallas as pl
@@ -15,6 +16,9 @@
 NX, NY, NZ = 8, 32, 128
 ROWS = NX * NY
 GX, GY, GZ = 8, 4, 8
+NEAR = [(-1, 0, 0), (1, 0, 0)] + [
+    (0, dy, dz) for dy in (-1, 1, 0) for dz in (-1, 1, 0) if (dy, dz) != (0, 0)
+]
 
 
 def gll_tables():
@@ -120,7 +124,28 @@
             1.0 / myz,
         ]
     )
-    return [np.asarray(t, np.float32) for t in (y_first, y_second, z_all)]
+    bf16 = ml_dtypes.bfloat16
+
+    def split(matrix):
+        high = np.asarray(matrix, np.float32).astype(bf16)
+        low = (matrix - high.astype(np.float64)).astype(np.float32).astype(bf16)
+        return high, low
+
+    y_first = np.concatenate(split(y_first), axis=0)
+    high, low = split(along(D, NZ).T)
+    z_first = np.concatenate(
+        [
+            np.concatenate([high, low], axis=1),
+            np.concatenate([high, np.zeros_like(low)], axis=1),
+        ],
+        axis=0,
+    )
+    return [
+        y_first,
+        z_first,
+        np.asarray(y_second, np.float32),
+        np.asarray(z_all, np.float32),
+    ]
 
 
 Y_AVG, Y_DA, Y_DF, Y_LA, Y_LF = 0, 256, 512, 528, 784
@@ -177,19 +202,22 @@
     adj,
     pen,
     yfirst,
+    zfirst,
     ysecond,
     zall,
-    projected,
-    pressure,
+    adv_out,
+    grad_out,
+    vec_out,
+    coef_out,
     bs,
     us,
     ps,
     y1,
+    z1,
     y2,
     zt,
     raw,
-    za,
-    ya,
+    halo,
     adv,
     pav,
     vec,
@@ -200,8 +228,13 @@
     rz1,
     fy1,
     ry1,
+    xf,
+    xq,
     rx1,
-    rxp,
+    rq1,
+    rx2,
+    hx1,
+    rmix,
     fx,
     rx,
     fy,
@@ -218,6 +251,7 @@
     red1,
     part,
     red2,
+    coef,
     load_sem,
     send_sem,
     recv_sem,
@@ -229,14 +263,21 @@
     py = lax.axis_index("gy")
     pz = lax.axis_index("gz")
 
+    def at(dx, dy, dz):
+        return (
+            lax.rem(px + dx + GX, GX),
+            lax.rem(py + dy + GY, GY),
+            lax.rem(pz + dz + GZ, GZ),
+        )
+
     def at_x(offset):
-        return (lax.rem(px + offset + GX, GX), py, pz)
+        return at(offset, 0, 0)
 
     def at_y(offset):
-        return (px, lax.rem(py + offset + GY, GY), pz)
+        return at(0, offset, 0)
 
     def at_z(offset):
-        return (px, py, lax.rem(pz + offset + GZ, GZ))
+        return at(0, 0, offset)
 
     row = px // 2
     half = lax.rem(px, 2)
@@ -255,22 +296,26 @@
         pltpu.make_async_copy(adj, us, load_sem.at[0]),
         pltpu.make_async_copy(base, bs, load_sem.at[1]),
         pltpu.make_async_copy(yfirst, y1, load_sem.at[2]),
-        pltpu.make_async_copy(zall, zt, load_sem.at[3]),
-        pltpu.make_async_copy(pen, ps, load_sem.at[4]),
-        pltpu.make_async_copy(ysecond, y2, load_sem.at[5]),
+        pltpu.make_async_copy(zfirst, z1, load_sem.at[3]),
+        pltpu.make_async_copy(zall, zt, load_sem.at[4]),
+        pltpu.make_async_copy(pen, ps, load_sem.at[5]),
+        pltpu.make_async_copy(ysecond, y2, load_sem.at[6]),
     ]
     for copy in loads:
         copy.start()
 
     barrier = pltpu.get_barrier_semaphore()
+    for dx, dy, dz in NEAR:
+        pl.semaphore_signal(
+            barrier, inc=1, device_id=at(dx, dy, dz), device_id_type=MESH
+        )
     for k in range(1, 16):
         pl.semaphore_signal(barrier, inc=1, device_id=group1(k), device_id_type=MESH)
         pl.semaphore_signal(barrier, inc=1, device_id=group2(k), device_id_type=MESH)
-    for k in (-1, 1):
-        pl.semaphore_signal(barrier, inc=1, device_id=at_x(k), device_id_type=MESH)
 
     hx = (jnp.where(px > 0, 0.5, 0.0), jnp.where(px < GX - 1, 0.5, 0.0))
     hy = (jnp.where(py > 0, 0.5, 0.0), jnp.where(py < GY - 1, 0.5, 0.0))
+    hx2 = (jnp.where(px > 1, 0.5, 0.0), jnp.where(px < GX - 2, 0.5, 0.0))
     sub = lax.broadcasted_iota(jnp.int32, (8, NZ), 0)
     first = jnp.where(sub == 0, 1.0, 0.0)
     last = jnp.where(sub == 7, 1.0, 0.0)
@@ -299,16 +344,32 @@
     def tiles(ref, yt):
         return [ref[x, pl.ds(8 * yt, 8), :] for x in range(NX)]
 
-    dz_table = zt[pl.ds(Z_D, 128), :]
+    def bf16_dot(a, b):
+        return lax.dot_general(
+            a, b, (((1,), (0,)), ((), ())), preferred_element_type=F32
+        )
+
+    def first_yz(value, need_y, need_z):
+        value = flat(value)
+        high = value.astype(jnp.bfloat16)
+        low = (value - high.astype(F32)).astype(jnp.bfloat16)
+        both = jnp.concatenate([high, low], axis=1)
+        dy = dz = None
+        if need_y:
+            out = bf16_dot(y1[...], both)
+            dy = cube(out[:ROWS, :NZ] + out[:ROWS, NZ:] + out[ROWS:, :NZ])
+        if need_z:
+            out = bf16_dot(both, z1[...])
+            dz = cube(out[:, :NZ] + out[:, NZ:])
+        return dy, dz
+
     for i in range(3):
-        ui = us.at[i]
-        dy = cube(dot(y1[...], flat(ui[...])))
-        dz = cube(dot(flat(ui[...]), dz_table))
+        dy, dz = first_yz(us[i], True, True)
         raw[i] = -(bs[1] * dy + bs[2] * dz)
     for j in range(3):
-        uj = bs.at[j]
-        raw[1] += us[j] * cube(dot(y1[...], flat(uj[...])))
-        raw[2] += us[j] * cube(dot(flat(uj[...]), dz_table))
+        dy, dz = first_yz(bs[j], True, True)
+        raw[1] += us[j] * dy
+        raw[2] += us[j] * dz
     for yt in range(4):
         rows = pl.ds(8 * yt, 8)
         for i in range(3):
@@ -319,65 +380,37 @@
             src = tiles(bs.at[j], yt)
             for x in range(NX):
                 raw[0, x, rows, :] += us[j, x, rows, :] * line(D[x], src)
-    loads[4].wait()
+    for copy in loads[4:6]:
+        copy.wait()
     raw[3] = ps[...]
-
-    avg_z = zt[pl.ds(Z_AVG, 128), :]
     pick = zt[pl.ds(Z_PICK, 16), :]
     faces = None
     for i in range(4):
         own = dot_nt(pick, flat(raw[i]))
-        if i == 0:
-            faces = own
-        else:
-            faces = faces + pltpu.roll(own, i, 0)
+        faces = own if i == 0 else faces + pltpu.roll(own, i, 0)
     fz1[...] = faces
-    pl.semaphore_wait(barrier, 32)
-    copies = [
-        send(fz1.at[pl.ds(0, 8)], rz1.at[pl.ds(8, 8)], at_z(-1)),
-        send(fz1.at[pl.ds(8, 8)], rz1.at[pl.ds(0, 8)], at_z(1)),
-    ]
-    for i in range(4):
-        za[i] = cube(dot(flat(raw[i]), avg_z))
-    for copy in copies:
-        copy.wait_recv()
-    delta = 0.5 * (rz1[...] - fz1[...])
-    for i in range(4):
-        pick_i = pick if i == 0 else pltpu.roll(pick, i, 0)
-        za[i] += cube(dot_tn(delta, pick_i))
-    loads[5].wait()
     for i in range(4):
         for x in range(NX):
-            fy1[0, i, pl.ds(x, 1), :] = za[i, x, pl.ds(0, 1), :]
-            fy1[1, i, pl.ds(x, 1), :] = za[i, x, pl.ds(NY - 1, 1), :]
-    copies = [
+            for side, y in ((0, 0), (1, NY - 1)):
+                fy1[side, i, pl.ds(x, 1), :] = raw[i, x, pl.ds(y, 1), :]
+    pl.semaphore_wait(barrier, 30 + len(NEAR))
+    near = []
+    for dz in (-1, 1):
+        for dy in (0, -1, 1):
+            src = fz1.at[pl.ds(0 if dz < 0 else 8, 8)]
+            dst = rz1.at[1 if dz < 0 else 0, 1 - dy]
+            near.append(send(src, dst, at(0, dy, dz)))
+    near += [
         send(fy1.at[0], ry1.at[1], at_y(-1)),
         send(fy1.at[1], ry1.at[0], at_y(1)),
     ]
-    avg_y = y2[pl.ds(Y_AVG, 256), :]
-    for i in range(4):
-        ya[i] = cube(dot(avg_y, flat(za[i])))
-    for copy in copies:
-        copy.wait_recv()
-
-    def add_y(target, low, high):
-        for x in range(NX):
-            target[x, pl.ds(0, 8), :] += first * low[x : x + 1, :]
-            target[x, pl.ds(NY - 8, 8), :] += last * high[x : x + 1, :]
-
-    for i in range(4):
-        add_y(
-            ya.at[i],
-            hy[0] * (ry1[0, i] - fy1[0, i]),
-            hy[1] * (ry1[1, i] - fy1[1, i]),
-        )
-    copies = [
-        send(ya.at[pl.ds(0, 3), 0], rx1.at[1], at_x(-1)),
-        send(ya.at[pl.ds(0, 3), NX - 1], rx1.at[0], at_x(1)),
+    raw_x = [
+        send(raw.at[pl.ds(0, 3), 0], rx1.at[1, pl.ds(0, 3)], at_x(-1)),
+        send(raw.at[pl.ds(0, 3), NX - 1], rx1.at[0, pl.ds(0, 3)], at_x(1)),
     ]
     copies_p = [
-        send(ya.at[3, 0], rxp.at[1], at_x(-1)),
-        send(ya.at[3, NX - 1], rxp.at[0], at_x(1)),
+        send(raw.at[3, 0], rx1.at[1, 3], at_x(-1)),
+        send(raw.at[3, NX - 1], rx1.at[0, 3], at_x(1)),
     ]
 
     w_tile = zt[pl.ds(Z_W, 8), :]
@@ -396,15 +429,161 @@
         for x in range(NX):
             wm[x, pl.ds(8 * yt, 8), :] = wm_y[yt] * (mult_x[x] * scale_x[x])
 
+    lane = lax.broadcasted_iota(jnp.int32, (8, NZ), 1)
+    begin = lax.rem(lane, 8) == 0
+    end = lax.rem(lane, 8) == 7
+    keep_z = jnp.where(begin | end, 0.5, 1.0)
+    from_low = jnp.where(begin & (lane > 0), 0.5, 0.0)
+    from_high = jnp.where(end & (lane < NZ - 1), 0.5, 0.0)
+    low_y = [first * hy[0]] + [first * 0.5] * 3
+    high_y = [last * 0.5] * 3 + [last * hy[1]]
+    keep_y = [1.0 - low_y[t] - high_y[t] for t in range(4)]
+
+    def mix_slab(src, low, high, edge, dst):
+        for t in range(4):
+            rows = pl.ds(8 * t, 8)
+            down = low if t == 0 else src[pl.ds(8 * t - 1, 1), :]
+            up = high if t == 3 else src[pl.ds(8 * t + 8, 1), :]
+            value = src[rows, :] * keep_y[t] + down * low_y[t] + up * high_y[t]
+            dst[rows, :] = (
+                value * keep_z
+                + pltpu.roll(value, 1, 1) * from_low
+                + pltpu.roll(value, NZ - 1, 1) * from_high
+                + edge[rows, :]
+            )
+
+    wide = lax.broadcasted_iota(jnp.int32, (8, ROWS), 1)
+    y_of = lax.rem(wide, NY)
+    x_of = wide // NY
+    inner_begin = (lax.rem(wide, 8) == 0) & (y_of > 0)
+    inner_end = (lax.rem(wide, 8) == 7) & (y_of < NY - 1)
+
+    def y_mix(mid, down, up):
+        partner = jnp.where(
+            y_of == 0,
+            pltpu.roll(down, ROWS - (NY - 1), 1),
+            jnp.where(
+                y_of == NY - 1,
+                pltpu.roll(up, NY - 1, 1),
+                jnp.where(
+                    inner_begin, pltpu.roll(mid, 1, 1), pltpu.roll(mid, ROWS - 1, 1)
+                ),
+            ),
+        )
+        weight = jnp.where(
+            y_of == 0,
+            hy[0],
+            jnp.where(
+                y_of == NY - 1, hy[1], jnp.where(inner_begin | inner_end, 0.5, 0.0)
+            ),
+        )
+        return mid + weight * (partner - mid)
+
+    spots = jnp.concatenate(
+        [
+            jnp.where((sub == i) & (lane == 0), 0.5, 0.0)
+            + jnp.where((sub == 4 + i) & (lane == NZ - 1), 0.5, 0.0)
+            for i in range(4)
+        ],
+        axis=1,
+    ).astype(F32)
+    spots = jnp.concatenate([spots] * 3, axis=0).astype(jnp.bfloat16)
+
+    def expand(values):
+        parts, rest = [], values
+        for _ in range(3):
+            parts.append(rest.astype(jnp.bfloat16).astype(F32))
+            rest = rest - parts[-1]
+        split = jnp.concatenate(parts, axis=0).astype(jnp.bfloat16)
+        return lax.dot_general(
+            split, spots, (((0,), (0,)), ((), ())), preferred_element_type=F32
+        )
+
+    for copy in near:
+        copy.wait_recv()
+    edges = y_mix(rz1[0, 1], rz1[0, 0], rz1[0, 2]) + pltpu.roll(
+        y_mix(rz1[1, 1], rz1[1, 0], rz1[1, 2]), 4, 0
+    )
+    wide_halo = expand(edges)
+    for i in range(4):
+        halo[i] = cube(wide_halo[:, NZ * i : NZ * (i + 1)])
+    for side in (0, 1):
+        for i in range(4):
+            for end in (0, 1):
+                xq[side, pl.ds(NY + 4 * end + i, 1), :] = ry1[
+                    end, i, pl.ds(side * (NX - 1), 1), :
+                ]
+        xq[side, pl.ds(NY + 8, 8), :] = edges[:, NZ * side : NZ * (side + 1)]
+
+    def mixed(i, x, dst):
+        mix_slab(
+            raw.at[i, x],
+            ry1[0, i, pl.ds(x, 1), :],
+            ry1[1, i, pl.ds(x, 1), :],
+            halo.at[i, x],
+            dst,
+        )
+
+    for side in (0, 1):
+        mixed(0, side * (NX - 1), xf.at[side, 0])
+    for x in range(1, NX - 1):
+        mixed(0, x, adv.at[0, x])
+    for yt in range(4):
+        rows = pl.ds(8 * yt, 8)
+        src = [xf[0, 0, rows, :]]
+        src += [adv[0, x, rows, :] for x in range(1, NX - 1)]
+        src += [xf[1, 0, rows, :]]
+        ends = [src[0] * (1.0 - hx[0]), src[NX - 1] * (1.0 - hx[1])]
+        xq[0, rows, :] = line(D[0], src[: NX - 1] + [ends[1]])
+        xq[1, rows, :] = line(D[NX - 1], [ends[0]] + src[1:])
+    sx = [
+        send(xq.at[0], rq1.at[1], at_x(-1)),
+        send(xq.at[1], rq1.at[0], at_x(1)),
+        send(xf.at[0, 0], rx2.at[1, 0], at_x(-2)),
+        send(xf.at[1, 0], rx2.at[0, 0], at_x(2)),
+    ]
+    for i in range(1, 3):
+        for side in (0, 1):
+            mixed(i, side * (NX - 1), xf.at[side, i])
+        for x in range(1, NX - 1):
+            mixed(i, x, adv.at[i, x])
+    for side in (0, 1):
+        mixed(3, side * (NX - 1), xf.at[side, 3])
+    for x in range(1, NX - 1):
+        mixed(3, x, pav.at[x])
+    loads[6].wait()
+    for copy in raw_x:
+        copy.wait_recv()
+    for copy in sx:
+        copy.wait_recv()
+    edges = jnp.where(lane < NZ // 2, rq1[1, pl.ds(NY + 8, 8), :], rq1[0, pl.ds(NY + 8, 8), :])
+    wide_halo = expand(edges)
+    for i in range(4):
+        part_halo = wide_halo[:, NZ * i : NZ * (i + 1)]
+        hx1[0, i] = part_halo[NZ - NY :, :]
+        hx1[1, i] = part_halo[:NY, :]
+
+    def neighbour_face(side, i):
+        mix_slab(
+            rx1.at[side, i],
+            rq1[side, pl.ds(NY + i, 1), :],
+            rq1[side, pl.ds(NY + 4 + i, 1), :],
+            hx1.at[side, i],
+            rmix.at[side, i],
+        )
+
     for i in range(3):
-        for x in range(1, NX - 1):
-            adv[i, x] = ya[i, x]
-    for copy in copies:
-        copy.wait_recv()
-    for i in range(3):
-        adv[i, 0] = ya[i, 0] + hx[0] * (rx1[0, i] - ya[i, 0])
-        adv[i, NX - 1] = ya[i, NX - 1] + hx[1] * (rx1[1, i] - ya[i, NX - 1])
-
+        for side in (0, 1):
+            neighbour_face(side, i)
+            own = xf[side, i]
+            adv[i, side * (NX - 1)] = own + hx[side] * (rmix[side, i] - own)
+    for side in (0, 1):
+        mine, other = side * (NX - 1), (1 - side) * (NX - 1)
+        rx[0, side] = (
+            rq1[side, pl.ds(0, NY), :]
+            + (0.5 * float(D[other, other])) * (xf[side, 0] - rmix[side, 0])
+            + (float(D[other, mine]) * hx2[side]) * rx2[side, 0]
+        )
     def local(vx, vy, vz, mx, ymat, zmat, with_mass):
         yz = cube(dot(y2[pl.ds(ymat, 256), :], flat(vy[...]))) + cube(
             dot(flat(vz[...]), zt[pl.ds(zmat, 128), :])
@@ -423,15 +602,60 @@
             low[pl.ds(8 * yt, 8), :] = line(mx[0], src)
             high[pl.ds(8 * yt, 8), :] = line(mx[NX - 1], src)
 
+    def add_y(target, low, high):
+        for x in range(NX):
+            target[x, pl.ds(0, 8), :] += first * low[x : x + 1, :]
+            target[x, pl.ds(NY - 8, 8), :] += last * high[x : x + 1, :]
+
     def add_z(target, delta_z):
         target[...] += cube(dot_tn(delta_z, pick))
 
+    gradient_copies = {}
+
+    def gradient_faces(k):
+        v = vec.at[k]
+        x_faces(v, D, gfx.at[0, k], gfx.at[1, k])
+        gfy[k] = dot(y2[pl.ds(Y_DF, 16), :], flat(v[...]))
+        gfz[k] = dot_nt(zt[pl.ds(Z_DF, 16), :], flat(v[...]))
+        low, high = pl.ds(0, 8), pl.ds(8, 8)
+        gradient_copies[k] = [
+            send(gfx.at[0, k], grx.at[1, k], at_x(-1)),
+            send(gfx.at[1, k], grx.at[0, k], at_x(1)),
+            send(gfz.at[k, low], grz.at[k, high], at_z(-1)),
+            send(gfz.at[k, high], grz.at[k, low], at_z(1)),
+            send(gfy.at[k, low], gry.at[k, high], at_y(-1)),
+            send(gfy.at[k, high], gry.at[k, low], at_y(1)),
+        ]
+
+    def gradient_local(k):
+        v = vec.at[k]
+        grad[k, 1] = cube(dot(y2[pl.ds(Y_DA, 256), :], flat(v[...])))
+        grad[k, 2] = cube(dot(flat(v[...]), zt[pl.ds(Z_DA, 128), :]))
+        for yt in range(4):
+            src = tiles(v, yt)
+            for x in range(NX):
+                grad[k, 0, x, pl.ds(8 * yt, 8), :] = line(D[x], src)
+
+    def gradient_edges(k):
+        for copy in gradient_copies[k]:
+            copy.wait_recv()
+        for side in (0, 1):
+            grad[k, 0, side * (NX - 1)] += hx[side] * (grx[side, k] - gfx[side, k])
+        add_y(
+            grad.at[k, 1],
+            hy[0] * (gry[k, pl.ds(0, 8), :] - gfy[k, pl.ds(0, 8), :]),
+            hy[1] * (gry[k, pl.ds(8, 8), :] - gfy[k, pl.ds(8, 8), :]),
+        )
+        add_z(grad.at[k, 2], 0.5 * (grz[k] - gfz[k]))
+
     def phase(k, vx, vy, vz, mx, ymat, yface, zmat, zface, with_mass, sign):
         x_faces(vx, mx, fx.at[k, 0], fx.at[k, 1])
-        sx = [
-            send(fx.at[k, 0], rx.at[k, 1], at_x(-1)),
-            send(fx.at[k, 1], rx.at[k, 0], at_x(1)),
-        ]
+        sx = []
+        if k > 0:
+            sx = [
+                send(fx.at[k, 0], rx.at[k, 1], at_x(-1)),
+                send(fx.at[k, 1], rx.at[k, 0], at_x(1)),
+            ]
         fz[k] = dot_nt(zt[pl.ds(zface, 16), :], flat(vz[...]))
         sz = [
             send(fz.at[k, pl.ds(0, 8)], rz.at[k, pl.ds(8, 8)], at_z(-1)),
@@ -445,6 +669,8 @@
         if with_mass and k == 1:
             finish_penalty()
         local(vx, vy, vz, mx, ymat, zmat, with_mass)
+        if k > 0:
+            gradient_faces(k - 1)
         for copy in sy:
             copy.wait_recv()
         add_y(
@@ -458,18 +684,20 @@
         out = vec.at[k]
         for x in range(1, NX - 1):
             out[x] = tt[x] * (sign * wm[x])
+        if k > 0:
+            gradient_local(k - 1)
         for copy in sx:
             copy.wait_recv()
         out[0] = (tt[0] + hx[0] * (rx[k, 0] - fx[k, 0])) * (sign * wm[0])
         out[NX - 1] = (tt[NX - 1] + hx[1] * (rx[k, 1] - fx[k, 1])) * (sign * wm[NX - 1])
 
     def finish_penalty():
-        for x in range(1, NX - 1):
-            pav[x] = ya[3, x]
         for copy in copies_p:
             copy.wait_recv()
-        pav[0] = ya[3, 0] + hx[0] * (rxp[0] - ya[3, 0])
-        pav[NX - 1] = ya[3, NX - 1] + hx[1] * (rxp[1] - ya[3, NX - 1])
+        for side in (0, 1):
+            neighbour_face(side, 3)
+            own = xf[side, 3]
+            pav[side * (NX - 1)] = own + hx[side] * (rmix[side, 3] - own)
 
     phase(0, adv.at[0], adv.at[1], adv.at[2], D, Y_DA, Y_DF, Z_DA, Z_DF, False, -1.0)
     for k in (1, 2):
@@ -532,48 +760,20 @@
 
     spread(mom, red1, index1, group1, 0)
 
-    zpick = zt[pl.ds(Z_DF, 16), :]
-    for k in range(3):
-        v = vec.at[k]
-        x_faces(v, D, gfx.at[0, k], gfx.at[1, k])
-        gfy[:, k] = dot(y2[pl.ds(Y_DF, 16), :], flat(v[...])).reshape(2, 8, NZ)
-    faces = None
-    for k in range(3):
-        own = dot_nt(zpick, flat(vec[k]))
-        faces = own if k == 0 else faces + pltpu.roll(own, k, 0)
-    gfz[...] = faces
-    gsend = [
-        send(gfx.at[0], grx.at[1], at_x(-1)),
-        send(gfx.at[1], grx.at[0], at_x(1)),
-        send(gfz.at[pl.ds(0, 8)], grz.at[pl.ds(8, 8)], at_z(-1)),
-        send(gfz.at[pl.ds(8, 8)], grz.at[pl.ds(0, 8)], at_z(1)),
-        send(gfy.at[0], gry.at[1], at_y(-1)),
-        send(gfy.at[1], gry.at[0], at_y(1)),
-    ]
+    gradient_faces(2)
     part[...] = gather(red1, 0)
     spread(part, red2, index2, group2, 1)
+    gradient_local(2)
     for k in range(3):
-        v = vec.at[k]
-        grad[k, 1] = cube(dot(y2[pl.ds(Y_DA, 256), :], flat(v[...])))
-        grad[k, 2] = cube(dot(flat(v[...]), zt[pl.ds(Z_DA, 128), :]))
-        for yt in range(4):
-            src = tiles(v, yt)
-            for x in range(NX):
-                grad[k, 0, x, pl.ds(8 * yt, 8), :] = line(D[x], src)
-    for copy in gsend:
-        copy.wait_recv()
-    delta_z = 0.5 * (grz[...] - gfz[...])
-    for k in range(3):
-        grad[k, 0, 0] += hx[0] * (grx[0, k] - gfx[0, k])
-        grad[k, 0, NX - 1] += hx[1] * (grx[1, k] - gfx[1, k])
-        add_y(
-            grad.at[k, 1],
-            hy[0] * (gry[0, k] - gfy[0, k]),
-            hy[1] * (gry[1, k] - gfy[1, k]),
-        )
-        pick_k = pick if k == 0 else pltpu.roll(pick, k, 0)
-        grad[k, 2] += cube(dot_tn(delta_z, pick_k))
-
+        gradient_edges(k)
+
+    outs = [
+        pltpu.make_async_copy(adv, adv_out, out_sem.at[0]),
+        pltpu.make_async_copy(grad, grad_out, out_sem.at[1]),
+        pltpu.make_async_copy(vec, vec_out, out_sem.at[2]),
+    ]
+    for copy in outs:
+        copy.start()
     sums = jnp.sum(gather(red2, 1), axis=1, keepdims=True)
     m = [jnp.broadcast_to(sums[k : k + 1, :], (8, NZ)) for k in range(6)]
     s0, s1, s2 = lax.rsqrt(m[1]), lax.rsqrt(m[3]), lax.rsqrt(m[5])
@@ -596,26 +796,70 @@
     c0 = y0 / h00 - l10 * c1 - l20 * c2
     c0, c1, c2 = c0 * s0, c1 * s1, c2 * s2
 
-    for yt in range(4):
-        rows = pl.ds(8 * yt, 8)
-        for x in range(NX):
-            tt[x, rows, :] = (
-                c0 * v0[x, rows, :] + c1 * v1[x, rows, :] + c2 * v2[x, rows, :]
-            )
-            for i in range(3):
-                raw[i, x, rows, :] = adv[i, x, rows, :] - (
-                    c0 * grad[0, i, x, rows, :]
-                    + c1 * grad[1, i, x, rows, :]
-                    + c2 * grad[2, i, x, rows, :]
-                )
-    outs = [
-        pltpu.make_async_copy(raw.at[pl.ds(0, 3)], projected, out_sem.at[0]),
-        pltpu.make_async_copy(tt, pressure, out_sem.at[1]),
-    ]
-    for copy in outs:
-        copy.start()
+    coef[...] = jnp.where(sub == 0, c0, jnp.where(sub == 1, c1, c2))
+    last_out = pltpu.make_async_copy(coef, coef_out, out_sem.at[3])
+    last_out.start()
     for copy in pending:
         copy.wait_send()
+    for copy in outs:
+        copy.wait()
+    last_out.wait()
+
+
+PIECES = 4
+
+
+def combine(
+    adv_in,
+    grad_in,
+    vec_in,
+    coef_in,
+    projected,
+    pressure,
+    adv,
+    grad,
+    vec,
+    coef,
+    proj,
+    pres,
+    load_sem,
+    coef_sem,
+    out_sem,
+):
+    size = NX // PIECES
+    coef_copy = pltpu.make_async_copy(coef_in, coef, coef_sem.at[0])
+    coef_copy.start()
+    loads, outs = [], []
+    for k in range(PIECES):
+        part = pl.ds(size * k, size)
+        copies = [
+            pltpu.make_async_copy(vec_in.at[:, part], vec.at[:, part], load_sem.at[k, 0]),
+            pltpu.make_async_copy(adv_in.at[:, part], adv.at[:, part], load_sem.at[k, 1]),
+            pltpu.make_async_copy(
+                grad_in.at[:, :, part], grad.at[:, :, part], load_sem.at[k, 2]
+            ),
+        ]
+        for copy in copies:
+            copy.start()
+        loads.append(copies)
+    coef_copy.wait()
+    c = [coef[pl.ds(k, 1), :] for k in range(3)]
+    for k in range(PIECES):
+        part = pl.ds(size * k, size)
+        loads[k][0].wait()
+        pres[part] = c[0] * vec[0, part] + c[1] * vec[1, part] + c[2] * vec[2, part]
+        outs.append(pltpu.make_async_copy(pres.at[part], pressure.at[part], out_sem.at[k, 0]))
+        outs[-1].start()
+        for copy in loads[k][1:]:
+            copy.wait()
+        for i in range(3):
+            proj[i, part] = adv[i, part] - (
+                c[0] * grad[0, i, part] + c[1] * grad[1, i, part] + c[2] * grad[2, i, part]
+            )
+        outs.append(
+            pltpu.make_async_copy(proj.at[:, part], projected.at[:, part], out_sem.at[k, 1])
+        )
+        outs[-1].start()
     for copy in outs:
         copy.wait()
 
@@ -625,23 +869,25 @@
     v = lambda *shape: pltpu.VMEM(shape, F32)
     consts = [jnp.asarray(t) for t in tables()]
     any_spec = pl.BlockSpec(memory_space=pltpu.HBM)
-    sends = 30
-    return pl.pallas_call(
+    sends = 60
+    adv, grad, vec, coef = pl.pallas_call(
         kernel,
         out_shape=(
             jax.ShapeDtypeStruct((3,) + field, F32),
-            jax.ShapeDtypeStruct(field, F32),
+            jax.ShapeDtypeStruct((3, 3) + field, F32),
+            jax.ShapeDtypeStruct((3,) + field, F32),
+            jax.ShapeDtypeStruct((8, NZ), F32),
         ),
-        in_specs=[any_spec] * 6,
-        out_specs=(any_spec, any_spec),
+        in_specs=[any_spec] * 7,
+        out_specs=(any_spec,) * 4,
         scratch_shapes=[
             v(3, *field),
             v(3, *field),
             v(*field),
-            v(*consts[0].shape),
-            v(*consts[1].shape),
+            pltpu.VMEM(consts[0].shape, jnp.bfloat16),
+            pltpu.VMEM(consts[1].shape, jnp.bfloat16),
             v(*consts[2].shape),
-            v(4, *field),
+            v(*consts[3].shape),
             v(4, *field),
             v(4, *field),
             v(3, *field),
@@ -651,11 +897,16 @@
             v(3, 3, *field),
             v(*field),
             v(16, ROWS),
-            v(16, ROWS),
+            v(2, 3, 8, ROWS),
             v(2, 4, 8, NZ),
             v(2, 4, 8, NZ),
-            v(2, 3, NY, NZ),
-            v(2, NY, NZ),
+            v(2, 4, NY, NZ),
+            v(2, NY + 16, NZ),
+            v(2, 4, NY, NZ),
+            v(2, NY + 16, NZ),
+            v(2, 2, NY, NZ),
+            v(2, 4, NY, NZ),
+            v(2, 4, NY, NZ),
             v(3, 2, NY, NZ),
             v(3, 2, NY, NZ),
             v(3, 16, NZ),
@@ -664,26 +915,49 @@
             v(3, 16, ROWS),
             v(2, 3, NY, NZ),
             v(2, 3, NY, NZ),
-            v(2, 3, 8, NZ),
-            v(2, 3, 8, NZ),
-            v(16, ROWS),
-            v(16, ROWS),
+            v(3, 16, NZ),
+            v(3, 16, NZ),
+            v(3, 16, ROWS),
+            v(3, 16, ROWS),
             v(8, NZ),
             v(16, 8, NZ),
             v(8, NZ),
             v(16, 8, NZ),
-            pltpu.SemaphoreType.DMA((6,)),
+            v(8, NZ),
+            pltpu.SemaphoreType.DMA((7,)),
             pltpu.SemaphoreType.DMA((sends + 10,)),
             pltpu.SemaphoreType.DMA((sends + 10,)),
             pltpu.SemaphoreType.DMA((2, 16)),
             pltpu.SemaphoreType.DMA((2,)),
-            pltpu.SemaphoreType.DMA((2,)),
+            pltpu.SemaphoreType.DMA((4,)),
         ],
         compiler_params=pltpu.CompilerParams(
             collective_id=0, has_side_effects=True, vmem_limit_bytes=63 * 1024 * 1024
         ),
         name="adjoint",
     )(base_flow, adjoint_velocity, penalty, *consts)
+    return pl.pallas_call(
+        combine,
+        out_shape=(
+            jax.ShapeDtypeStruct((3,) + field, F32),
+            jax.ShapeDtypeStruct(field, F32),
+        ),
+        in_specs=[any_spec] * 4,
+        out_specs=(any_spec,) * 2,
+        scratch_shapes=[
+            v(3, *field),
+            v(3, 3, *field),
+            v(3, *field),
+            v(8, NZ),
+            v(3, *field),
+            v(*field),
+            pltpu.SemaphoreType.DMA((PIECES, 3)),
+            pltpu.SemaphoreType.DMA((1,)),
+            pltpu.SemaphoreType.DMA((PIECES, 2)),
+        ],
+        compiler_params=pltpu.CompilerParams(vmem_limit_bytes=63 * 1024 * 1024),
+        name="combine",
+    )(adv, grad, vec, coef)
 
 
 def solution(mesh):

time: 59.4 us -> 55.1 us (0.928)
  local copies, waits for them, and re-layouts: 2.46 us -> 0 us
  Pallas kernels: 56.1 us -> 54.3 us
    pallas_call x1, Pallas kernels: 56.1 us -> 51.9 us  [per_device(): pl.pallas_call(kernel, out_shape=(jax.ShapeDtypeStruct((3,) + field, F32)...]
    unnamed x4 -> x0, local copies, waits for them, and re-layouts: 2.46 us -> none
    pallas_call x0 -> x1, Pallas kernels: none -> 2.39 us  [per_device(): pl.pallas_call(combine, out_shape=(jax.ShapeDtypeStruct((3,) + field, F32...]
where the time goes in v2:
time: 55.1 us; the launch traced here: 55 us
  Pallas kernels  54.3 us (99%)
  between operations  0.64 us (1%)
    pallas_call x1, Pallas kernels, per_device(): pl.pallas_call(kernel, out_shape=(jax.ShapeDtypeStruct((3,) + field, F32)...  51.9 us
    pallas_call x1, Pallas kernels, per_device(): pl.pallas_call(combine, out_shape=(jax.ShapeDtypeStruct((3,) + field, F32...  2.39 us

profile of v2, /device:TPU:1, one launch (start us, length us, event | category | flops | bytes accessed | tf_op | source)
XLA Modules:
  0.0 55.0 jit_solution(5852270265658867394)
XLA Ops:
  0.6 51.9 %adjoint.1 = (f32[3,8,32,128]{3,2,1,0:T(8,128)}, f32[3,3,8,32,128]{4,3,2,1,0:T(8,128)}, f32[3,8,32,128]{3,2,1,0:T(8,128)}, f32[8,128]{1,0:T(8,128)}) custom-call(f32[3,8,32,128]{3,2,1,0:T(8,128)} %base.1, f32[3,8,32,128]{3,2,1,0:T(8,128)} %adj.1, f32[8,32,128]{2,1,0:T(8,128)} %pen.1, bf16[512,256]{1,0:T(8,128)(2,1)} %constant.8.clone.yfirst, ...), custom_call_target="tpu_custom_call" | custom-call | tf_op jit(solution)/shard_map/adjoint/pallas_call | solution.py:873
  52.6 2.4 %combine.1 = (f32[3,8,32,128]{3,2,1,0:T(8,128)}, f32[8,32,128]{2,1,0:T(8,128)}) custom-call(f32[3,8,32,128]{3,2,1,0:T(8,128)} %get-tuple-element.6.adv_in, f32[3,3,8,32,128]{4,3,2,1,0:T(8,128)} %get-tuple-element.7.grad_in, f32[3,8,32,128]{3,2,1,0:T(8,128)} %get-tuple-element.8.vec_in, f32[8,128]{1,0:T(8,128)} %get-tuple-element.9.coef_in), custom_call_target="tpu_custom_call" | custom-call | tf_op jit(solution)/shard_map/combine/pallas_call | solution.py:939

commit v3 on v2

--- a/solution.py
+++ b/solution.py
@@ -11,7 +11,6 @@
 
 MESH = pl.DeviceIdType.MESH
 F32 = jnp.float32
-HI = lax.Precision.HIGHEST
 N = 8
 NX, NY, NZ = 8, 32, 128
 ROWS = NX * NY
@@ -70,19 +69,6 @@
     return np.kron(np.eye(extent // 8), matrix)
 
 
-def over_y(matrix):
-    return np.kron(np.eye(NX), matrix)
-
-
-def face_rows_y(matrix):
-    rows = np.zeros((16, ROWS))
-    full = along(matrix, NY)
-    for x in range(NX):
-        rows[x, x * NY : (x + 1) * NY] = full[0]
-        rows[8 + x, x * NY : (x + 1) * NY] = full[NY - 1]
-    return rows
-
-
 def face_rows_z(matrix):
     rows = np.zeros((16, NZ))
     full = along(matrix, NZ)
@@ -91,94 +77,81 @@
     return rows
 
 
+def split(matrix):
+    parts, rest = [], np.asarray(matrix, np.float64)
+    for _ in range(3):
+        parts.append(rest.astype(np.float32).astype(ml_dtypes.bfloat16))
+        rest = rest - parts[-1].astype(np.float64)
+    return parts
+
+
 def tables():
-    ay, az = average(NY), average(NZ)
-    y_first = over_y(along(D, NY))
-    y_second = np.concatenate(
-        [
-            over_y(ay),
-            over_y(ay @ along(D, NY)),
-            face_rows_y(D),
-            over_y(ay @ along(L, NY)),
-            face_rows_y(L),
-        ]
+    az = average(NZ)
+    blocks = []
+    for matrix in (along(D, NZ), az @ along(D, NZ), az @ along(L, NZ)):
+        high, mid, low = split(matrix.T)
+        blocks.append(
+            np.concatenate(
+                [
+                    np.concatenate([high, mid, high], axis=1),
+                    np.concatenate([high, mid, low], axis=1),
+                ],
+                axis=0,
+            )
+        )
+    z_blocks = np.stack(blocks)
+    picks = np.zeros((16, NZ))
+    picks[0, 0] = 1.0
+    picks[8, NZ - 1] = 1.0
+    z_faces = np.concatenate(
+        split(face_rows_z(D))
+        + split(face_rows_z(L))
+        + [picks.astype(ml_dtypes.bfloat16)] * 3,
+        axis=0,
     )
     local = np.arange(8)
     edge = np.where((local == 0) | (local == 7), 2.0, 1.0)
     wyz = W[:, None] * np.tile(W, 16)[None, :]
     myz = edge[:, None] * np.tile(edge, 16)[None, :]
-    picks = np.zeros((16, NZ))
-    picks[0, 0] = 1.0
-    picks[8, NZ - 1] = 1.0
-    z_all = np.concatenate(
-        [
-            along(D, NZ).T,
-            az.T,
-            (az @ along(D, NZ)).T,
-            (az @ along(L, NZ)).T,
-            face_rows_z(D),
-            face_rows_z(L),
-            picks,
-            wyz,
-            wyz * myz,
-            1.0 / myz,
-        ]
-    )
-    bf16 = ml_dtypes.bfloat16
-
-    def split(matrix):
-        high = np.asarray(matrix, np.float32).astype(bf16)
-        low = (matrix - high.astype(np.float64)).astype(np.float32).astype(bf16)
-        return high, low
-
-    y_first = np.concatenate(split(y_first), axis=0)
-    high, low = split(along(D, NZ).T)
-    z_first = np.concatenate(
-        [
-            np.concatenate([high, low], axis=1),
-            np.concatenate([high, np.zeros_like(low)], axis=1),
-        ],
-        axis=0,
-    )
-    return [
-        y_first,
-        z_first,
-        np.asarray(y_second, np.float32),
-        np.asarray(z_all, np.float32),
+    columns = [
+        np.repeat(matrix[:, k : k + 1], NZ, axis=1)
+        for matrix in (D, L)
+        for k in range(8)
     ]
-
-
-Y_AVG, Y_DA, Y_DF, Y_LA, Y_LF = 0, 256, 512, 528, 784
-Z_D, Z_AVG, Z_DA, Z_LA, Z_DF, Z_LF, Z_PICK, Z_W, Z_WM, Z_IM = (
-    0,
-    128,
-    256,
-    384,
-    512,
-    528,
-    544,
-    560,
-    568,
-    576,
-)
+    small = np.concatenate([wyz, wyz * myz, 1.0 / myz] + columns, axis=0)
+    return [z_blocks, z_faces, np.asarray(small, np.float32)]
+
+
+Z_D, Z_DA, Z_LA = 0, 1, 2
+F_D, F_L, F_PICK = 0, 48, 96
+T_W, T_WM, T_IM, T_D, T_L = 0, 8, 16, 24, 88
 
 
 def dot(a, b):
-    return lax.dot_general(
-        a, b, (((1,), (0,)), ((), ())), precision=HI, preferred_element_type=F32
-    )
+    return lax.dot_general(a, b, (((1,), (0,)), ((), ())), preferred_element_type=F32)
 
 
 def dot_nt(a, b):
-    return lax.dot_general(
-        a, b, (((1,), (1,)), ((), ())), precision=HI, preferred_element_type=F32
-    )
+    return lax.dot_general(a, b, (((1,), (1,)), ((), ())), preferred_element_type=F32)
 
 
 def dot_tn(a, b):
-    return lax.dot_general(
-        a, b, (((0,), (0,)), ((), ())), precision=HI, preferred_element_type=F32
-    )
+    return lax.dot_general(a, b, (((0,), (0,)), ((), ())), preferred_element_type=F32)
+
+
+def split3(value):
+    high = value.astype(jnp.bfloat16)
+    rest = value - high.astype(F32)
+    mid = rest.astype(jnp.bfloat16)
+    return high, mid, (rest - mid.astype(F32)).astype(jnp.bfloat16)
+
+
+def stack3(value):
+    parts, rest = [], value
+    for _ in range(3):
+        parts.append(rest.astype(jnp.bfloat16).astype(F32))
+        rest = rest - parts[-1]
+    return jnp.concatenate(parts, axis=0).astype(jnp.bfloat16)
 
 
 def flat(value):
@@ -201,10 +174,9 @@
     base,
     adj,
     pen,
-    yfirst,
-    zfirst,
-    ysecond,
-    zall,
+    zblocks,
+    zfaces,
+    small,
     adv_out,
     grad_out,
     vec_out,
@@ -212,9 +184,8 @@
     bs,
     us,
     ps,
-    y1,
-    z1,
-    y2,
+    zb,
+    zf,
     zt,
     raw,
     halo,
@@ -224,6 +195,9 @@
     tt,
     grad,
     wm,
+    wyz,
+    q2,
+    rq2,
     fz1,
     rz1,
     fy1,
@@ -295,11 +269,13 @@
     loads = [
         pltpu.make_async_copy(adj, us, load_sem.at[0]),
         pltpu.make_async_copy(base, bs, load_sem.at[1]),
-        pltpu.make_async_copy(yfirst, y1, load_sem.at[2]),
-        pltpu.make_async_copy(zfirst, z1, load_sem.at[3]),
-        pltpu.make_async_copy(zall, zt, load_sem.at[4]),
+        pltpu.make_async_copy(zblocks.at[0], zb.at[0], load_sem.at[2]),
+        pltpu.make_async_copy(small, zt, load_sem.at[3]),
+        pltpu.make_async_copy(zfaces, zf, load_sem.at[4]),
         pltpu.make_async_copy(pen, ps, load_sem.at[5]),
-        pltpu.make_async_copy(ysecond, y2, load_sem.at[6]),
+        pltpu.make_async_copy(
+            zblocks.at[pl.ds(1, 2)], zb.at[pl.ds(1, 2)], load_sem.at[6]
+        ),
     ]
     for copy in loads:
         copy.start()
@@ -341,37 +317,62 @@
     for copy in loads[:4]:
         copy.wait()
 
+    def y_rows(yt):
+        return pl.ds(8 * yt, 8)
+
     def tiles(ref, yt):
-        return [ref[x, pl.ds(8 * yt, 8), :] for x in range(NX)]
-
-    def bf16_dot(a, b):
-        return lax.dot_general(
-            a, b, (((1,), (0,)), ((), ())), preferred_element_type=F32
-        )
-
-    def first_yz(value, need_y, need_z):
-        value = flat(value)
-        high = value.astype(jnp.bfloat16)
-        low = (value - high.astype(F32)).astype(jnp.bfloat16)
-        both = jnp.concatenate([high, low], axis=1)
-        dy = dz = None
-        if need_y:
-            out = bf16_dot(y1[...], both)
-            dy = cube(out[:ROWS, :NZ] + out[:ROWS, NZ:] + out[ROWS:, :NZ])
-        if need_z:
-            out = bf16_dot(both, z1[...])
-            dz = cube(out[:, :NZ] + out[:, NZ:])
-        return dy, dz
-
+        return [ref[x, y_rows(yt), :] for x in range(NX)]
+
+    def loop(count, start=0):
+        def run(body):
+            for k in range(start, count):
+                body(k)
+
+        return run
+
+    def columns(offset):
+        return [zt[pl.ds(offset + 8 * k, 8), :] for k in range(8)]
+
+    def y_line(ref, x, coefficients):
+        result = []
+        for t in range(4):
+            total = None
+            for k in range(8):
+                part = coefficients[k] * ref[x, pl.ds(8 * t + k, 1), :]
+                total = part if total is None else total + part
+            result.append(total)
+        return result
+
+    def z_line(parts, block):
+        high, mid, low = parts
+        out = dot(
+            jnp.concatenate([high, mid], axis=1), zb[block, :, pl.ds(0, 2 * NZ)]
+        )
+        rest = dot(
+            jnp.concatenate([low, high], axis=1), zb[block, :, pl.ds(2 * NZ, NZ)]
+        )
+        return cube(out[:, :NZ] + (out[:, NZ:] + rest))
+
+    d_columns = columns(T_D)
     for i in range(3):
-        dy, dz = first_yz(us[i], True, True)
-        raw[i] = -(bs[1] * dy + bs[2] * dz)
+        raw[i] = -bs[2] * z_line(split3(flat(us[i])), Z_D)
     for j in range(3):
-        dy, dz = first_yz(bs[j], True, True)
-        raw[1] += us[j] * dy
-        raw[2] += us[j] * dz
-    for yt in range(4):
-        rows = pl.ds(8 * yt, 8)
+        raw[2] += us[j] * z_line(split3(flat(bs[j])), Z_D)
+
+    @loop(NX)
+    def _(x):
+        for i in range(3):
+            for t, value in enumerate(y_line(us.at[i], x, d_columns)):
+                rows = pl.ds(8 * t, 8)
+                raw[i, x, rows, :] -= bs[1, x, rows, :] * value
+        for j in range(3):
+            for t, value in enumerate(y_line(bs.at[j], x, d_columns)):
+                rows = pl.ds(8 * t, 8)
+                raw[1, x, rows, :] += us[j, x, rows, :] * value
+
+    @loop(4)
+    def _(yt):
+        rows = y_rows(yt)
         for i in range(3):
             src = tiles(us.at[i], yt)
             for x in range(NX):
@@ -380,13 +381,25 @@
             src = tiles(bs.at[j], yt)
             for x in range(NX):
                 raw[0, x, rows, :] += us[j, x, rows, :] * line(D[x], src)
+
     for copy in loads[4:6]:
         copy.wait()
     raw[3] = ps[...]
-    pick = zt[pl.ds(Z_PICK, 16), :]
+    def z_faces(parts, offset):
+        high, mid, low = parts
+        table = zf[pl.ds(offset, 48), :]
+        a, b = dot_nt(table, high), dot_nt(table[:32], mid)
+        c = dot_nt(table[:16], low)
+        return a[:16] + (a[16:32] + b[:16] + (a[32:] + b[16:] + c))
+
+    def z_ends(parts):
+        table = zf[pl.ds(F_PICK, 16), :]
+        a, b, c = (dot_nt(table, part) for part in parts)
+        return a + (b + c)
+
     faces = None
     for i in range(4):
-        own = dot_nt(pick, flat(raw[i]))
+        own = z_ends(split3(flat(raw[i])))
         faces = own if i == 0 else faces + pltpu.roll(own, i, 0)
     fz1[...] = faces
     for i in range(4):
@@ -413,9 +426,9 @@
         send(raw.at[3, NX - 1], rx1.at[0, 3], at_x(1)),
     ]
 
-    w_tile = zt[pl.ds(Z_W, 8), :]
-    wm_tile = zt[pl.ds(Z_WM, 8), :]
-    im_tile = zt[pl.ds(Z_IM, 8), :]
+    w_tile = zt[pl.ds(T_W, 8), :]
+    wm_tile = zt[pl.ds(T_WM, 8), :]
+    im_tile = zt[pl.ds(T_IM, 8), :]
     fix_low = 1.0 - first * (0.5 - hy[0])
     fix_high = 1.0 - last * (0.5 - hy[1])
     inv_low = 1.0 + first * (1.0 - 2.0 * hy[0])
@@ -428,6 +441,7 @@
     for yt in range(4):
         for x in range(NX):
             wm[x, pl.ds(8 * yt, 8), :] = wm_y[yt] * (mult_x[x] * scale_x[x])
+        wyz[pl.ds(8 * yt, 8), :] = wm_y[yt]
 
     lane = lax.broadcasted_iota(jnp.int32, (8, NZ), 1)
     begin = lax.rem(lane, 8) == 0
@@ -490,14 +504,7 @@
     spots = jnp.concatenate([spots] * 3, axis=0).astype(jnp.bfloat16)
 
     def expand(values):
-        parts, rest = [], values
-        for _ in range(3):
-            parts.append(rest.astype(jnp.bfloat16).astype(F32))
-            rest = rest - parts[-1]
-        split = jnp.concatenate(parts, axis=0).astype(jnp.bfloat16)
-        return lax.dot_general(
-            split, spots, (((0,), (0,)), ((), ())), preferred_element_type=F32
-        )
+        return dot_tn(stack3(values), spots)
 
     for copy in near:
         copy.wait_recv()
@@ -526,31 +533,36 @@
 
     for side in (0, 1):
         mixed(0, side * (NX - 1), xf.at[side, 0])
-    for x in range(1, NX - 1):
+    @loop(NX - 1, 1)
+    def _(x):
         mixed(0, x, adv.at[0, x])
-    for yt in range(4):
-        rows = pl.ds(8 * yt, 8)
+
+    @loop(4)
+    def _(yt):
+        rows = y_rows(yt)
         src = [xf[0, 0, rows, :]]
         src += [adv[0, x, rows, :] for x in range(1, NX - 1)]
         src += [xf[1, 0, rows, :]]
         ends = [src[0] * (1.0 - hx[0]), src[NX - 1] * (1.0 - hx[1])]
         xq[0, rows, :] = line(D[0], src[: NX - 1] + [ends[1]])
         xq[1, rows, :] = line(D[NX - 1], [ends[0]] + src[1:])
+
     sx = [
         send(xq.at[0], rq1.at[1], at_x(-1)),
         send(xq.at[1], rq1.at[0], at_x(1)),
         send(xf.at[0, 0], rx2.at[1, 0], at_x(-2)),
         send(xf.at[1, 0], rx2.at[0, 0], at_x(2)),
     ]
-    for i in range(1, 3):
+    for i in range(1, 4):
         for side in (0, 1):
             mixed(i, side * (NX - 1), xf.at[side, i])
-        for x in range(1, NX - 1):
+
+    @loop(NX - 1, 1)
+    def _(x):
+        for i in range(1, 3):
             mixed(i, x, adv.at[i, x])
-    for side in (0, 1):
-        mixed(3, side * (NX - 1), xf.at[side, 3])
-    for x in range(1, NX - 1):
         mixed(3, x, pav.at[x])
+
     loads[6].wait()
     for copy in raw_x:
         copy.wait_recv()
@@ -584,23 +596,42 @@
             + (0.5 * float(D[other, other])) * (xf[side, 0] - rmix[side, 0])
             + (float(D[other, mine]) * hx2[side]) * rx2[side, 0]
         )
-    def local(vx, vy, vz, mx, ymat, zmat, with_mass):
-        yz = cube(dot(y2[pl.ds(ymat, 256), :], flat(vy[...]))) + cube(
-            dot(flat(vz[...]), zt[pl.ds(zmat, 128), :])
-        )
-        if with_mass:
-            yz = yz + pav[...] * vx[...]
-        tt[...] = yz
-        for yt in range(4):
-            src = tiles(vx, yt)
+    inner_low, inner_high = first * 0.5, last * 0.5
+    keep_inner = [
+        1.0 - (inner_low if t > 0 else 0.0) - (inner_high if t < 3 else 0.0)
+        for t in range(4)
+    ]
+
+    def y_part(ref, offset, target, faces):
+        coefficients = columns(offset)
+
+        @loop(NX)
+        def _(x):
+            values = y_line(ref, x, coefficients)
+            if faces is not None:
+                faces[pl.ds(x, 1), :] = values[0][:1, :]
+                faces[pl.ds(8 + x, 1), :] = values[3][7:, :]
+            for t in range(4):
+                value = values[t] * keep_inner[t]
+                if t > 0:
+                    value = value + pltpu.roll(values[t - 1], 1, 0) * inner_low
+                if t < 3:
+                    value = value + pltpu.roll(values[t + 1], 7, 0) * inner_high
+                target[x, pl.ds(8 * t, 8), :] = value
+
+    def x_part(ref, mx, target):
+        @loop(4)
+        def _(yt):
+            src = tiles(ref, yt)
             for x in range(NX):
-                tt[x, pl.ds(8 * yt, 8), :] += line(mx[x], src)
+                target[x, y_rows(yt), :] += line(mx[x], src)
 
     def x_faces(source, mx, low, high):
-        for yt in range(4):
+        @loop(4)
+        def _(yt):
             src = tiles(source, yt)
-            low[pl.ds(8 * yt, 8), :] = line(mx[0], src)
-            high[pl.ds(8 * yt, 8), :] = line(mx[NX - 1], src)
+            low[y_rows(yt), :] = line(mx[0], src)
+            high[y_rows(yt), :] = line(mx[NX - 1], src)
 
     def add_y(target, low, high):
         for x in range(NX):
@@ -608,15 +639,26 @@
             target[x, pl.ds(NY - 8, 8), :] += last * high[x : x + 1, :]
 
     def add_z(target, delta_z):
-        target[...] += cube(dot_tn(delta_z, pick))
+        target[...] += cube(dot_tn(stack3(delta_z), zf[pl.ds(F_PICK, 48), :]))
 
     gradient_copies = {}
 
-    def gradient_faces(k):
+    def gradient(k):
         v = vec.at[k]
-        x_faces(v, D, gfx.at[0, k], gfx.at[1, k])
-        gfy[k] = dot(y2[pl.ds(Y_DF, 16), :], flat(v[...]))
-        gfz[k] = dot_nt(zt[pl.ds(Z_DF, 16), :], flat(v[...]))
+        parts = split3(flat(v[...]))
+        gfz[k] = z_faces(parts, F_D)
+        y_part(v, T_D, grad.at[k, 1], gfy.at[k])
+
+        @loop(4)
+        def _(yt):
+            rows = y_rows(yt)
+            src = tiles(v, yt)
+            for x in range(NX):
+                value = line(D[x], src)
+                grad[k, 0, x, rows, :] = value
+                if x in (0, NX - 1):
+                    gfx[min(x, 1), k, rows, :] = value
+
         low, high = pl.ds(0, 8), pl.ds(8, 8)
         gradient_copies[k] = [
             send(gfx.at[0, k], grx.at[1, k], at_x(-1)),
@@ -626,15 +668,7 @@
             send(gfy.at[k, low], gry.at[k, high], at_y(-1)),
             send(gfy.at[k, high], gry.at[k, low], at_y(1)),
         ]
-
-    def gradient_local(k):
-        v = vec.at[k]
-        grad[k, 1] = cube(dot(y2[pl.ds(Y_DA, 256), :], flat(v[...])))
-        grad[k, 2] = cube(dot(flat(v[...]), zt[pl.ds(Z_DA, 128), :]))
-        for yt in range(4):
-            src = tiles(v, yt)
-            for x in range(NX):
-                grad[k, 0, x, pl.ds(8 * yt, 8), :] = line(D[x], src)
+        grad[k, 2] = z_line(parts, Z_DA)
 
     def gradient_edges(k):
         for copy in gradient_copies[k]:
@@ -648,29 +682,40 @@
         )
         add_z(grad.at[k, 2], 0.5 * (grz[k] - gfz[k]))
 
-    def phase(k, vx, vy, vz, mx, ymat, yface, zmat, zface, with_mass, sign):
+    far = []
+
+    def phase(k, vx, vy, vz, mx, ycol, zmat, zface, with_mass, sign):
         x_faces(vx, mx, fx.at[k, 0], fx.at[k, 1])
         sx = []
-        if k > 0:
+        if k == 1:
             sx = [
                 send(fx.at[k, 0], rx.at[k, 1], at_x(-1)),
                 send(fx.at[k, 1], rx.at[k, 0], at_x(1)),
             ]
-        fz[k] = dot_nt(zt[pl.ds(zface, 16), :], flat(vz[...]))
+            far[:] = [
+                send(fx.at[k, 0], rx2.at[1, 1], at_x(-2)),
+                send(fx.at[k, 1], rx2.at[0, 1], at_x(2)),
+            ]
+        parts = split3(flat(vz[...]))
+        fz[k] = z_faces(parts, zface)
         sz = [
             send(fz.at[k, pl.ds(0, 8)], rz.at[k, pl.ds(8, 8)], at_z(-1)),
             send(fz.at[k, pl.ds(8, 8)], rz.at[k, pl.ds(0, 8)], at_z(1)),
         ]
-        fy[k] = dot(y2[pl.ds(yface, 16), :], flat(vy[...]))
+        y_part(vy, ycol, tt, fy.at[k])
         sy = [
             send(fy.at[k, pl.ds(0, 8)], ry.at[k, pl.ds(8, 8)], at_y(-1)),
             send(fy.at[k, pl.ds(8, 8)], ry.at[k, pl.ds(0, 8)], at_y(1)),
         ]
         if with_mass and k == 1:
             finish_penalty()
-        local(vx, vy, vz, mx, ymat, zmat, with_mass)
-        if k > 0:
-            gradient_faces(k - 1)
+        rest = z_line(parts, zmat)
+        if with_mass:
+            rest = rest + pav[...] * vx[...]
+        tt[...] += rest
+        x_part(vx, mx, tt)
+        if k > 1:
+            gradient(k - 1)
         for copy in sy:
             copy.wait_recv()
         add_y(
@@ -684,8 +729,36 @@
         out = vec.at[k]
         for x in range(1, NX - 1):
             out[x] = tt[x] * (sign * wm[x])
-        if k > 0:
-            gradient_local(k - 1)
+        if k == 1:
+            @loop(4)
+            def _(yt):
+                rows = y_rows(yt)
+                src = [tt[0, rows, :] * wm[0, rows, :]]
+                src += [out[x, rows, :] for x in range(1, NX - 1)]
+                src += [tt[NX - 1, rows, :] * wm[NX - 1, rows, :]]
+                weight = wyz[rows, :]
+                below = fx[1, 0, rows, :] * weight * (2.0 * scale_x[0] * hx[0])
+                above = fx[1, 1, rows, :] * weight * (2.0 * scale_x[-1] * hx[1])
+                q2[0, rows, :] = line(L[0], src[:-1] + [src[-1] - above])
+                q2[1, rows, :] = line(L[NX - 1], [src[0] - below] + src[1:])
+
+            far[2:] = [
+                send(q2.at[0], rq2.at[1], at_x(-1)),
+                send(q2.at[1], rq2.at[0], at_x(1)),
+            ]
+            gradient(0)
+        if k == 2:
+            for copy in far:
+                copy.wait_recv()
+            for side in (0, 1):
+                mine, other = side * (NX - 1), (1 - side) * (NX - 1)
+                near_term = (scale_x[other] * float(L[other, other])) * (
+                    fx[1, side] - rx[1, side]
+                )
+                far_term = (2.0 * scale_x[mine] * float(L[other, mine])) * hx2[side]
+                rx[2, side] = rq2[side] + wyz[...] * (
+                    near_term + far_term * rx2[side, 1]
+                )
         for copy in sx:
             copy.wait_recv()
         out[0] = (tt[0] + hx[0] * (rx[k, 0] - fx[k, 0])) * (sign * wm[0])
@@ -699,10 +772,10 @@
             own = xf[side, 3]
             pav[side * (NX - 1)] = own + hx[side] * (rmix[side, 3] - own)
 
-    phase(0, adv.at[0], adv.at[1], adv.at[2], D, Y_DA, Y_DF, Z_DA, Z_DF, False, -1.0)
+    phase(0, adv.at[0], adv.at[1], adv.at[2], D, T_D, Z_DA, F_D, False, -1.0)
     for k in (1, 2):
         v = vec.at[k - 1]
-        phase(k, v, v, v, L, Y_LA, Y_LF, Z_LA, Z_LF, True, 1.0)
+        phase(k, v, v, v, L, T_L, Z_LA, F_L, True, 1.0)
 
     def inner(a, b):
         total = None
@@ -719,7 +792,9 @@
         return jnp.sum(total, axis=0, keepdims=True)
 
     v0, v1, v2 = vec.at[0], vec.at[1], vec.at[2]
-    local(v2, v2, v2, L, Y_LA, Z_LA, True)
+    y_part(v2, T_L, tt, None)
+    tt[...] += z_line(split3(flat(vec[2])), Z_LA) + pav[...] * v2[...]
+    x_part(v2, L, tt)
     total = None
     for yt in range(4):
         rows = pl.ds(8 * yt, 8)
@@ -760,10 +835,9 @@
 
     spread(mom, red1, index1, group1, 0)
 
-    gradient_faces(2)
+    gradient(2)
     part[...] = gather(red1, 0)
     spread(part, red2, index2, group2, 1)
-    gradient_local(2)
     for k in range(3):
         gradient_edges(k)
 
@@ -878,7 +952,7 @@
             jax.ShapeDtypeStruct((3,) + field, F32),
             jax.ShapeDtypeStruct((8, NZ), F32),
         ),
-        in_specs=[any_spec] * 7,
+        in_specs=[any_spec] * 6,
         out_specs=(any_spec,) * 4,
         scratch_shapes=[
             v(3, *field),
@@ -887,7 +961,6 @@
             pltpu.VMEM(consts[0].shape, jnp.bfloat16),
             pltpu.VMEM(consts[1].shape, jnp.bfloat16),
             v(*consts[2].shape),
-            v(*consts[3].shape),
             v(4, *field),
             v(4, *field),
             v(3, *field),
@@ -896,6 +969,9 @@
             v(*field),
             v(3, 3, *field),
             v(*field),
+            v(NY, NZ),
+            v(2, NY, NZ),
+            v(2, NY, NZ),
             v(16, ROWS),
             v(2, 3, 8, ROWS),
             v(2, 4, 8, NZ),

time: 55.1 us -> 53.1 us (0.964)
  Pallas kernels: 54.3 us -> 52.3 us
    pallas_call x1, Pallas kernels: 51.9 us -> 50 us  [per_device(): pl.pallas_call(kernel, out_shape=(jax.ShapeDtypeStruct((3,) + field, F32)...]
where the time goes in v3:
time: 53.1 us; the launch traced here: 53 us
  Pallas kernels  52.3 us (98%)
  between operations  0.64 us (1%)
    pallas_call x1, Pallas kernels, per_device(): pl.pallas_call(kernel, out_shape=(jax.ShapeDtypeStruct((3,) + field, F32)...  50 us
    pallas_call x1, Pallas kernels, per_device(): pl.pallas_call(combine, out_shape=(jax.ShapeDtypeStruct((3,) + field, F32...  2.39 us

profile of v3, /device:TPU:1, one launch (start us, length us, event | category | flops | bytes accessed | tf_op | source)
XLA Modules:
  0.0 53.0 jit_solution(11339025221610652444)
XLA Ops:
  0.6 50.0 %adjoint.1 = (f32[3,8,32,128]{3,2,1,0:T(8,128)}, f32[3,3,8,32,128]{4,3,2,1,0:T(8,128)}, f32[3,8,32,128]{3,2,1,0:T(8,128)}, f32[8,128]{1,0:T(8,128)}) custom-call(f32[3,8,32,128]{3,2,1,0:T(8,128)} %base.1, f32[3,8,32,128]{3,2,1,0:T(8,128)} %adj.1, f32[8,32,128]{2,1,0:T(8,128)} %pen.1, bf16[3,256,384]{2,1,0:T(8,128)(2,1)} %constant.6.clone.zblocks, ...), custom_call_target="tpu_custom_call" | custom-call | tf_op jit(solution)/shard_map/adjoint/pallas_call | solution.py:947
  50.6 2.4 %combine.1 = (f32[3,8,32,128]{3,2,1,0:T(8,128)}, f32[8,32,128]{2,1,0:T(8,128)}) custom-call(f32[3,8,32,128]{3,2,1,0:T(8,128)} %get-tuple-element.6.adv_in, f32[3,3,8,32,128]{4,3,2,1,0:T(8,128)} %get-tuple-element.7.grad_in, f32[3,8,32,128]{3,2,1,0:T(8,128)} %get-tuple-element.8.vec_in, f32[8,128]{1,0:T(8,128)} %get-tuple-element.9.coef_in), custom_call_target="tpu_custom_call" | custom-call | tf_op jit(solution)/shard_map/combine/pallas_call | solution.py:1015

commit v4 on v3

--- a/solution.py
+++ b/solution.py
@@ -15,6 +15,7 @@
 NX, NY, NZ = 8, 32, 128
 ROWS = NX * NY
 GX, GY, GZ = 8, 4, 8
+PIECES = 4
 NEAR = [(-1, 0, 0), (1, 0, 0)] + [
     (0, dy, dz) for dy in (-1, 1, 0) for dz in (-1, 1, 0) if (dy, dz) != (0, 0)
 ]
@@ -177,10 +178,8 @@
     zblocks,
     zfaces,
     small,
-    adv_out,
-    grad_out,
-    vec_out,
-    coef_out,
+    projected,
+    pressure,
     bs,
     us,
     ps,
@@ -225,7 +224,7 @@
     red1,
     part,
     red2,
-    coef,
+    res,
     load_sem,
     send_sem,
     recv_sem,
@@ -285,9 +284,10 @@
         pl.semaphore_signal(
             barrier, inc=1, device_id=at(dx, dy, dz), device_id_type=MESH
         )
-    for k in range(1, 16):
-        pl.semaphore_signal(barrier, inc=1, device_id=group1(k), device_id_type=MESH)
-        pl.semaphore_signal(barrier, inc=1, device_id=group2(k), device_id_type=MESH)
+    mates1 = [group1(k) for k in range(1, 16)]
+    mates2 = [group2(k) for k in range(1, 16)]
+    for mate in mates1 + mates2:
+        pl.semaphore_signal(barrier, inc=1, device_id=mate, device_id_type=MESH)
 
     hx = (jnp.where(px > 0, 0.5, 0.0), jnp.where(px < GX - 1, 0.5, 0.0))
     hy = (jnp.where(py > 0, 0.5, 0.0), jnp.where(py < GY - 1, 0.5, 0.0))
@@ -410,8 +410,8 @@
     near = []
     for dz in (-1, 1):
         for dy in (0, -1, 1):
-            src = fz1.at[pl.ds(0 if dz < 0 else 8, 8)]
-            dst = rz1.at[1 if dz < 0 else 0, 1 - dy]
+            src = fz1.at[pl.ds(0 if dz < 0 else 8, 4)]
+            dst = rz1.at[1 if dz < 0 else 0, 1 - dy, pl.ds(0, 4)]
             near.append(send(src, dst, at(0, dy, dz)))
     near += [
         send(fy1.at[0], ry1.at[1], at_y(-1)),
@@ -421,11 +421,6 @@
         send(raw.at[pl.ds(0, 3), 0], rx1.at[1, pl.ds(0, 3)], at_x(-1)),
         send(raw.at[pl.ds(0, 3), NX - 1], rx1.at[0, pl.ds(0, 3)], at_x(1)),
     ]
-    copies_p = [
-        send(raw.at[3, 0], rx1.at[1, 3], at_x(-1)),
-        send(raw.at[3, NX - 1], rx1.at[0, 3], at_x(1)),
-    ]
-
     w_tile = zt[pl.ds(T_W, 8), :]
     wm_tile = zt[pl.ds(T_WM, 8), :]
     im_tile = zt[pl.ds(T_IM, 8), :]
@@ -508,8 +503,10 @@
 
     for copy in near:
         copy.wait_recv()
-    edges = y_mix(rz1[0, 1], rz1[0, 0], rz1[0, 2]) + pltpu.roll(
-        y_mix(rz1[1, 1], rz1[1, 0], rz1[1, 2]), 4, 0
+    edges = jnp.where(
+        lax.broadcasted_iota(jnp.int32, (8, ROWS), 0) < 4,
+        y_mix(rz1[0, 1], rz1[0, 0], rz1[0, 2]),
+        pltpu.roll(y_mix(rz1[1, 1], rz1[1, 0], rz1[1, 2]), 4, 0),
     )
     wide_halo = expand(edges)
     for i in range(4):
@@ -553,6 +550,10 @@
         send(xf.at[0, 0], rx2.at[1, 0], at_x(-2)),
         send(xf.at[1, 0], rx2.at[0, 0], at_x(2)),
     ]
+    copies_p = [
+        send(raw.at[3, 0], rx1.at[1, 3], at_x(-1)),
+        send(raw.at[3, NX - 1], rx1.at[0, 3], at_x(1)),
+    ]
     for i in range(1, 4):
         for side in (0, 1):
             mixed(i, side * (NX - 1), xf.at[side, i])
@@ -609,8 +610,8 @@
         def _(x):
             values = y_line(ref, x, coefficients)
             if faces is not None:
-                faces[pl.ds(x, 1), :] = values[0][:1, :]
-                faces[pl.ds(8 + x, 1), :] = values[3][7:, :]
+                faces[0, pl.ds(x, 1), :] = values[0][:1, :]
+                faces[1, pl.ds(x, 1), :] = values[3][7:, :]
             for t in range(4):
                 value = values[t] * keep_inner[t]
                 if t > 0:
@@ -641,13 +642,15 @@
     def add_z(target, delta_z):
         target[...] += cube(dot_tn(stack3(delta_z), zf[pl.ds(F_PICK, 48), :]))
 
-    gradient_copies = {}
-
     def gradient(k):
         v = vec.at[k]
         parts = split3(flat(v[...]))
-        gfz[k] = z_faces(parts, F_D)
-        y_part(v, T_D, grad.at[k, 1], gfy.at[k])
+        ends = z_faces(parts, F_D)
+        if k == 0:
+            gfz[...] = ends
+        else:
+            gfz[...] += pltpu.roll(ends, k, 0)
+        y_part(v, T_D, grad.at[k, 1], gfy.at[:, k])
 
         @loop(4)
         def _(yt):
@@ -659,32 +662,45 @@
                 if x in (0, NX - 1):
                     gfx[min(x, 1), k, rows, :] = value
 
-        low, high = pl.ds(0, 8), pl.ds(8, 8)
-        gradient_copies[k] = [
-            send(gfx.at[0, k], grx.at[1, k], at_x(-1)),
-            send(gfx.at[1, k], grx.at[0, k], at_x(1)),
-            send(gfz.at[k, low], grz.at[k, high], at_z(-1)),
-            send(gfz.at[k, high], grz.at[k, low], at_z(1)),
-            send(gfy.at[k, low], gry.at[k, high], at_y(-1)),
-            send(gfy.at[k, high], gry.at[k, low], at_y(1)),
+        grad[k, 2] = z_line(parts, Z_DA)
+
+    def gradient_edges():
+        delta = grz[...] - gfz[...]
+        wide_halo = expand(delta[:8] + pltpu.roll(delta[8:], 4, 0))
+        for k in range(3):
+            for side in (0, 1):
+                grad[k, 0, side * (NX - 1)] += hx[side] * (grx[side, k] - gfx[side, k])
+            add_y(
+                grad.at[k, 1],
+                hy[0] * (gry[0, k] - gfy[0, k]),
+                hy[1] * (gry[1, k] - gfy[1, k]),
+            )
+            grad[k, 2] += cube(wide_halo[:, NZ * k : NZ * (k + 1)])
+
+    def inner(a, b):
+        total = None
+        for yt in range(4):
+            rows = pl.ds(8 * yt, 8)
+            s = None
+            for x in range(NX):
+                p = a[x, rows, :] * b[x, rows, :]
+                if x in (0, NX - 1):
+                    p = p * inv_x[x]
+                s = p if s is None else s + p
+            s = s * im_y[yt]
+            total = s if total is None else total + s
+        return jnp.sum(total, axis=0, keepdims=True)
+
+    end_rows = lax.rem(lax.broadcasted_iota(jnp.int32, (16, ROWS), 0), 8) == 0
+    far = []
+
+    def phase(k, vx, vy, vz, mx, ycol, zmat, zface, with_mass, sign):
+        parts = split3(flat(vz[...]))
+        fz[k] = z_faces(parts, zface)
+        sz = [
+            send(fz.at[k, pl.ds(0, 1)], rz.at[k, pl.ds(8, 1)], at_z(-1)),
+            send(fz.at[k, pl.ds(8, 1)], rz.at[k, pl.ds(0, 1)], at_z(1)),
         ]
-        grad[k, 2] = z_line(parts, Z_DA)
-
-    def gradient_edges(k):
-        for copy in gradient_copies[k]:
-            copy.wait_recv()
-        for side in (0, 1):
-            grad[k, 0, side * (NX - 1)] += hx[side] * (grx[side, k] - gfx[side, k])
-        add_y(
-            grad.at[k, 1],
-            hy[0] * (gry[k, pl.ds(0, 8), :] - gfy[k, pl.ds(0, 8), :]),
-            hy[1] * (gry[k, pl.ds(8, 8), :] - gfy[k, pl.ds(8, 8), :]),
-        )
-        add_z(grad.at[k, 2], 0.5 * (grz[k] - gfz[k]))
-
-    far = []
-
-    def phase(k, vx, vy, vz, mx, ycol, zmat, zface, with_mass, sign):
         x_faces(vx, mx, fx.at[k, 0], fx.at[k, 1])
         sx = []
         if k == 1:
@@ -692,40 +708,39 @@
                 send(fx.at[k, 0], rx.at[k, 1], at_x(-1)),
                 send(fx.at[k, 1], rx.at[k, 0], at_x(1)),
             ]
+        y_part(vy, ycol, tt, fy.at[k])
+        sy = [
+            send(fy.at[k, 0], ry.at[k, 1], at_y(-1)),
+            send(fy.at[k, 1], ry.at[k, 0], at_y(1)),
+        ]
+        if with_mass and k == 1:
+            finish_penalty()
+        if k == 1:
             far[:] = [
                 send(fx.at[k, 0], rx2.at[1, 1], at_x(-2)),
                 send(fx.at[k, 1], rx2.at[0, 1], at_x(2)),
             ]
-        parts = split3(flat(vz[...]))
-        fz[k] = z_faces(parts, zface)
-        sz = [
-            send(fz.at[k, pl.ds(0, 8)], rz.at[k, pl.ds(8, 8)], at_z(-1)),
-            send(fz.at[k, pl.ds(8, 8)], rz.at[k, pl.ds(0, 8)], at_z(1)),
-        ]
-        y_part(vy, ycol, tt, fy.at[k])
-        sy = [
-            send(fy.at[k, pl.ds(0, 8)], ry.at[k, pl.ds(8, 8)], at_y(-1)),
-            send(fy.at[k, pl.ds(8, 8)], ry.at[k, pl.ds(0, 8)], at_y(1)),
-        ]
-        if with_mass and k == 1:
-            finish_penalty()
         rest = z_line(parts, zmat)
         if with_mass:
             rest = rest + pav[...] * vx[...]
         tt[...] += rest
         x_part(vx, mx, tt)
-        if k > 1:
-            gradient(k - 1)
+        if k == 2:
+            gradient(1)
+            mom[pl.ds(0, 1), :] = inner(vec.at[0], vec.at[0])
+            mom[pl.ds(1, 1), :] = inner(vec.at[0], vec.at[1])
+            mom[pl.ds(2, 1), :] = inner(vec.at[1], vec.at[1])
+            mom[pl.ds(6, 2), :] = jnp.zeros((2, NZ), F32)
         for copy in sy:
             copy.wait_recv()
         add_y(
             tt,
-            hy[0] * (ry[k, pl.ds(0, 8), :] - fy[k, pl.ds(0, 8), :]),
-            hy[1] * (ry[k, pl.ds(8, 8), :] - fy[k, pl.ds(8, 8), :]),
+            hy[0] * (ry[k, 0] - fy[k, 0]),
+            hy[1] * (ry[k, 1] - fy[k, 1]),
         )
         for copy in sz:
             copy.wait_recv()
-        add_z(tt, 0.5 * (rz[k] - fz[k]))
+        add_z(tt, jnp.where(end_rows, 0.5 * (rz[k] - fz[k]), 0.0))
         out = vec.at[k]
         for x in range(1, NX - 1):
             out[x] = tt[x] * (sign * wm[x])
@@ -777,20 +792,6 @@
         v = vec.at[k - 1]
         phase(k, v, v, v, L, T_L, Z_LA, F_L, True, 1.0)
 
-    def inner(a, b):
-        total = None
-        for yt in range(4):
-            rows = pl.ds(8 * yt, 8)
-            s = None
-            for x in range(NX):
-                p = a[x, rows, :] * b[x, rows, :]
-                if x in (0, NX - 1):
-                    p = p * inv_x[x]
-                s = p if s is None else s + p
-            s = s * im_y[yt]
-            total = s if total is None else total + s
-        return jnp.sum(total, axis=0, keepdims=True)
-
     v0, v1, v2 = vec.at[0], vec.at[1], vec.at[2]
     y_part(v2, T_L, tt, None)
     tt[...] += z_line(split3(flat(vec[2])), Z_LA) + pav[...] * v2[...]
@@ -804,50 +805,52 @@
             s = p if s is None else s + p
         total = s if total is None else total + s
     mom[pl.ds(5, 1), :] = jnp.sum(total * w_tile, axis=0, keepdims=True)
-    mom[pl.ds(0, 1), :] = inner(v0, v0)
-    mom[pl.ds(1, 1), :] = inner(v0, v1)
-    mom[pl.ds(2, 1), :] = inner(v1, v1)
     mom[pl.ds(3, 1), :] = inner(v1, v2)
     mom[pl.ds(4, 1), :] = inner(v2, v2)
-    mom[pl.ds(6, 2), :] = jnp.zeros((2, NZ), F32)
-
-    def spread(source, slots, own, group, which):
+
+    def spread(source, slots, own, mates, which):
         slots[own] = source[...]
-        for k in range(1, 16):
-            copy = pltpu.make_async_remote_copy(
+        for mate in mates:
+            pltpu.make_async_remote_copy(
                 src_ref=source,
                 dst_ref=slots.at[own],
-                send_sem=red_send.at[which, k],
+                send_sem=red_send.at[which],
                 recv_sem=red_recv.at[which],
-                device_id=group(k),
+                device_id=mate,
                 device_id_type=MESH,
-            )
-            copy.start()
-            pending.append(copy)
+            ).start()
+
+    def wait_all(slots, semaphore):
+        view = slots.at[pl.ds(0, 15)]
+        pltpu.make_async_copy(view, view, semaphore).wait()
 
     def gather(slots, which):
-        view = slots.at[pl.ds(0, 15)]
-        pltpu.make_async_copy(view, view, red_recv.at[which]).wait()
+        wait_all(slots, red_recv.at[which])
         total = slots[0]
         for k in range(1, 16):
             total = total + slots[k]
         return total
 
-    spread(mom, red1, index1, group1, 0)
+    spread(mom, red1, index2, mates2, 0)
 
     gradient(2)
+    gradient_copies = [
+        send(gfx.at[0], grx.at[1], at_x(-1)),
+        send(gfx.at[1], grx.at[0], at_x(1)),
+        send(gfz.at[pl.ds(0, 8)], grz.at[pl.ds(8, 8)], at_z(-1)),
+        send(gfz.at[pl.ds(8, 8)], grz.at[pl.ds(0, 8)], at_z(1)),
+        send(gfy.at[0], gry.at[1], at_y(-1)),
+        send(gfy.at[1], gry.at[0], at_y(1)),
+    ]
     part[...] = gather(red1, 0)
-    spread(part, red2, index2, group2, 1)
-    for k in range(3):
-        gradient_edges(k)
-
-    outs = [
-        pltpu.make_async_copy(adv, adv_out, out_sem.at[0]),
-        pltpu.make_async_copy(grad, grad_out, out_sem.at[1]),
-        pltpu.make_async_copy(vec, vec_out, out_sem.at[2]),
-    ]
-    for copy in outs:
-        copy.start()
+    spread(part, red2, index1, mates1, 1)
+    for copy in gradient_copies:
+        copy.wait_recv()
+    gradient_edges()
+
+    for copy in pending:
+        copy.wait_send()
+    wait_all(red1, red_send.at[0])
     sums = jnp.sum(gather(red2, 1), axis=1, keepdims=True)
     m = [jnp.broadcast_to(sums[k : k + 1, :], (8, NZ)) for k in range(6)]
     s0, s1, s2 = lax.rsqrt(m[1]), lax.rsqrt(m[3]), lax.rsqrt(m[5])
@@ -870,70 +873,47 @@
     c0 = y0 / h00 - l10 * c1 - l20 * c2
     c0, c1, c2 = c0 * s0, c1 * s1, c2 * s2
 
-    coef[...] = jnp.where(sub == 0, c0, jnp.where(sub == 1, c1, c2))
-    last_out = pltpu.make_async_copy(coef, coef_out, out_sem.at[3])
-    last_out.start()
-    for copy in pending:
-        copy.wait_send()
+    c0, c1, c2 = c0[:1], c1[:1], c2[:1]
+    outs = []
+    for k in range(PIECES):
+        slabs = pl.ds(k * (NX // PIECES), NX // PIECES)
+        tt[slabs] = c0 * v0[slabs] + c1 * v1[slabs] + c2 * v2[slabs]
+        outs.append(
+            pltpu.make_async_copy(tt.at[slabs], pressure.at[slabs], out_sem.at[k, 0])
+        )
+        outs[-1].start()
+        for i in range(3):
+            res[i, slabs] = adv[i, slabs] - (
+                c0 * grad[0, i, slabs] + c1 * grad[1, i, slabs] + c2 * grad[2, i, slabs]
+            )
+        outs.append(
+            pltpu.make_async_copy(
+                res.at[:, slabs], projected.at[:, slabs], out_sem.at[k, 1]
+            )
+        )
+        outs[-1].start()
+    wait_all(red2, red_send.at[1])
     for copy in outs:
         copy.wait()
-    last_out.wait()
-
-
-PIECES = 4
-
-
-def combine(
-    adv_in,
-    grad_in,
-    vec_in,
-    coef_in,
-    projected,
-    pressure,
-    adv,
-    grad,
-    vec,
-    coef,
-    proj,
-    pres,
-    load_sem,
-    coef_sem,
-    out_sem,
-):
-    size = NX // PIECES
-    coef_copy = pltpu.make_async_copy(coef_in, coef, coef_sem.at[0])
-    coef_copy.start()
+
+
+def hand_on(projected_in, pressure_in, projected, pressure, proj, pres, load_sem, sem):
     loads, outs = [], []
     for k in range(PIECES):
-        part = pl.ds(size * k, size)
-        copies = [
-            pltpu.make_async_copy(vec_in.at[:, part], vec.at[:, part], load_sem.at[k, 0]),
-            pltpu.make_async_copy(adv_in.at[:, part], adv.at[:, part], load_sem.at[k, 1]),
-            pltpu.make_async_copy(
-                grad_in.at[:, :, part], grad.at[:, :, part], load_sem.at[k, 2]
-            ),
-        ]
-        for copy in copies:
-            copy.start()
-        loads.append(copies)
-    coef_copy.wait()
-    c = [coef[pl.ds(k, 1), :] for k in range(3)]
-    for k in range(PIECES):
-        part = pl.ds(size * k, size)
-        loads[k][0].wait()
-        pres[part] = c[0] * vec[0, part] + c[1] * vec[1, part] + c[2] * vec[2, part]
-        outs.append(pltpu.make_async_copy(pres.at[part], pressure.at[part], out_sem.at[k, 0]))
-        outs[-1].start()
-        for copy in loads[k][1:]:
-            copy.wait()
-        for i in range(3):
-            proj[i, part] = adv[i, part] - (
-                c[0] * grad[0, i, part] + c[1] * grad[1, i, part] + c[2] * grad[2, i, part]
-            )
-        outs.append(
-            pltpu.make_async_copy(proj.at[:, part], projected.at[:, part], out_sem.at[k, 1])
-        )
-        outs[-1].start()
+        slabs = pl.ds(k * (NX // PIECES), NX // PIECES)
+        for i, (source, held, target) in enumerate(
+            [
+                (projected_in.at[:, slabs], proj.at[:, slabs], projected.at[:, slabs]),
+                (pressure_in.at[slabs], pres.at[slabs], pressure.at[slabs]),
+            ]
+        ):
+            loads.append(pltpu.make_async_copy(source, held, load_sem.at[k, i]))
+            outs.append(pltpu.make_async_copy(held, target, sem.at[k, i]))
+    for copy in loads:
+        copy.start()
+    for load, out in zip(loads, outs):
+        load.wait()
+        out.start()
     for copy in outs:
         copy.wait()
 
@@ -944,16 +924,15 @@
     consts = [jnp.asarray(t) for t in tables()]
     any_spec = pl.BlockSpec(memory_space=pltpu.HBM)
     sends = 60
-    adv, grad, vec, coef = pl.pallas_call(
+    shapes = (
+        jax.ShapeDtypeStruct((3,) + field, F32),
+        jax.ShapeDtypeStruct(field, F32),
+    )
+    results = pl.pallas_call(
         kernel,
-        out_shape=(
-            jax.ShapeDtypeStruct((3,) + field, F32),
-            jax.ShapeDtypeStruct((3, 3) + field, F32),
-            jax.ShapeDtypeStruct((3,) + field, F32),
-            jax.ShapeDtypeStruct((8, NZ), F32),
-        ),
+        out_shape=shapes,
         in_specs=[any_spec] * 6,
-        out_specs=(any_spec,) * 4,
+        out_specs=(any_spec,) * 2,
         scratch_shapes=[
             v(3, *field),
             v(3, *field),
@@ -985,27 +964,27 @@
             v(2, 4, NY, NZ),
             v(3, 2, NY, NZ),
             v(3, 2, NY, NZ),
-            v(3, 16, NZ),
-            v(3, 16, NZ),
+            v(3, 2, 8, NZ),
+            v(3, 2, 8, NZ),
             v(3, 16, ROWS),
             v(3, 16, ROWS),
             v(2, 3, NY, NZ),
             v(2, 3, NY, NZ),
-            v(3, 16, NZ),
-            v(3, 16, NZ),
-            v(3, 16, ROWS),
-            v(3, 16, ROWS),
+            v(2, 3, 8, NZ),
+            v(2, 3, 8, NZ),
+            v(16, ROWS),
+            v(16, ROWS),
             v(8, NZ),
             v(16, 8, NZ),
             v(8, NZ),
             v(16, 8, NZ),
-            v(8, NZ),
+            v(3, *field),
             pltpu.SemaphoreType.DMA((7,)),
             pltpu.SemaphoreType.DMA((sends + 10,)),
             pltpu.SemaphoreType.DMA((sends + 10,)),
-            pltpu.SemaphoreType.DMA((2, 16)),
             pltpu.SemaphoreType.DMA((2,)),
-            pltpu.SemaphoreType.DMA((4,)),
+            pltpu.SemaphoreType.DMA((2,)),
+            pltpu.SemaphoreType.DMA((PIECES, 2)),
         ],
         compiler_params=pltpu.CompilerParams(
             collective_id=0, has_side_effects=True, vmem_limit_bytes=63 * 1024 * 1024
@@ -1013,27 +992,19 @@
         name="adjoint",
     )(base_flow, adjoint_velocity, penalty, *consts)
     return pl.pallas_call(
-        combine,
-        out_shape=(
-            jax.ShapeDtypeStruct((3,) + field, F32),
-            jax.ShapeDtypeStruct(field, F32),
-        ),
-        in_specs=[any_spec] * 4,
+        hand_on,
+        out_shape=shapes,
+        in_specs=[any_spec] * 2,
         out_specs=(any_spec,) * 2,
         scratch_shapes=[
             v(3, *field),
-            v(3, 3, *field),
-            v(3, *field),
-            v(8, NZ),
-            v(3, *field),
             v(*field),
-            pltpu.SemaphoreType.DMA((PIECES, 3)),
-            pltpu.SemaphoreType.DMA((1,)),
+            pltpu.SemaphoreType.DMA((PIECES, 2)),
             pltpu.SemaphoreType.DMA((PIECES, 2)),
         ],
         compiler_params=pltpu.CompilerParams(vmem_limit_bytes=63 * 1024 * 1024),
-        name="combine",
-    )(adv, grad, vec, coef)
+        name="hand_on",
+    )(*results)
 
 
 def solution(mesh):

time: 53.1 us -> 51.3 us (0.966)
  Pallas kernels: 52.3 us -> 50.5 us
    pallas_call x2, Pallas kernels: 52.3 us -> 50.5 us  [the longest x1 48.7 us: per_device(): pl.pallas_call(kernel, out_shape=shapes, in_specs=[any_spec] * 6, out_spe...]
where the time goes in v4:
time: 51.3 us; the launch traced here: 51.2 us
  Pallas kernels  50.5 us (98%)
  between operations  0.64 us (1%)
    pallas_call x1, Pallas kernels, per_device(): pl.pallas_call(kernel, out_shape=shapes, in_specs=[any_spec] * 6, out_spe...  48.7 us
    pallas_call x1, Pallas kernels, per_device(): pl.pallas_call(hand_on, out_shape=shapes, in_specs=[any_spec] * 2, out_sp...  1.88 us

profile of v4, /device:TPU:1, one launch (start us, length us, event | category | flops | bytes accessed | tf_op | source)
XLA Modules:
  0.0 51.2 jit_solution(4021595886086874602)
XLA Ops:
  0.6 48.7 %adjoint.1 = (f32[3,8,32,128]{3,2,1,0:T(8,128)}, f32[8,32,128]{2,1,0:T(8,128)}) custom-call(f32[3,8,32,128]{3,2,1,0:T(8,128)} %base.1, f32[3,8,32,128]{3,2,1,0:T(8,128)} %adj.1, f32[8,32,128]{2,1,0:T(8,128)} %pen.1, bf16[3,256,384]{2,1,0:T(8,128)(2,1)} %constant.6.clone.zblocks, bf16[144,128]{1,0:T(8,128)(2,1)} %constant.7.clone.zfaces, ...), custom_call_target="tpu_custom_call" | custom-call | tf_op jit(solution)/shard_map/adjoint/pallas_call | solution.py:931
  49.3 1.9 %hand_on.1 = (f32[3,8,32,128]{3,2,1,0:T(8,128)}, f32[8,32,128]{2,1,0:T(8,128)}) custom-call(f32[3,8,32,128]{3,2,1,0:T(8,128)} %get-tuple-element.4.projected_in, f32[8,32,128]{2,1,0:T(8,128)} %get-tuple-element.5.pressure_in), custom_call_target="tpu_custom_call" | custom-call | tf_op jit(solution)/shard_map/hand_on/pallas_call | solution.py:994

commit v5 on v4

--- a/solution.py
+++ b/solution.py
@@ -862,9 +862,11 @@
     l10 = h01 / h00
     l20 = h02 / h00
     d1 = h11 - l10 * h01
+    d1 = jnp.where(d1 > 1e-6, d1, 1e30)
     e1 = h12 - l20 * h01
     l21 = e1 / d1
     d2 = h22 - l20 * h02 - l21 * e1
+    d2 = jnp.where(d2 > 1e-6, d2, 1e30)
     y0 = g0
     y1_ = g1 - l10 * y0
     y2_ = g2 - l20 * y0 - l21 * y1_

time: 51.3 us -> 51.3 us (level)
  no operation moved by 1% of the time
where the time goes in v5:
time: 51.3 us; the launch traced here: 51.2 us
  Pallas kernels  50.5 us (98%)
  between operations  0.64 us (1%)
    pallas_call x1, Pallas kernels, per_device(): pl.pallas_call(kernel, out_shape=shapes, in_specs=[any_spec] * 6, out_spe...  48.7 us
    pallas_call x1, Pallas kernels, per_device(): pl.pallas_call(hand_on, out_shape=shapes, in_specs=[any_spec] * 2, out_sp...  1.88 us

profile of v5, /device:TPU:1, one launch (start us, length us, event | category | flops | bytes accessed | tf_op | source)
XLA Modules:
  0.0 51.2 jit_solution(13268143180553115232)
XLA Ops:
  0.6 48.7 %adjoint.1 = (f32[3,8,32,128]{3,2,1,0:T(8,128)}, f32[8,32,128]{2,1,0:T(8,128)}) custom-call(f32[3,8,32,128]{3,2,1,0:T(8,128)} %base.1, f32[3,8,32,128]{3,2,1,0:T(8,128)} %adj.1, f32[8,32,128]{2,1,0:T(8,128)} %pen.1, bf16[3,256,384]{2,1,0:T(8,128)(2,1)} %constant.6.clone.zblocks, bf16[144,128]{1,0:T(8,128)(2,1)} %constant.7.clone.zfaces, ...), custom_call_target="tpu_custom_call" | custom-call | tf_op jit(solution)/shard_map/adjoint/pallas_call | solution.py:933
  49.3 1.9 %hand_on.1 = (f32[3,8,32,128]{3,2,1,0:T(8,128)}, f32[8,32,128]{2,1,0:T(8,128)}) custom-call(f32[3,8,32,128]{3,2,1,0:T(8,128)} %get-tuple-element.4.projected_in, f32[8,32,128]{2,1,0:T(8,128)} %get-tuple-element.5.pressure_in), custom_call_target="tpu_custom_call" | custom-call | tf_op jit(solution)/shard_map/hand_on/pallas_call | solution.py:996

commit v6 on v5

--- a/solution.py
+++ b/solution.py
@@ -15,7 +15,7 @@
 NX, NY, NZ = 8, 32, 128
 ROWS = NX * NY
 GX, GY, GZ = 8, 4, 8
-PIECES = 4
+PIECES = 2
 NEAR = [(-1, 0, 0), (1, 0, 0)] + [
     (0, dy, dz) for dy in (-1, 1, 0) for dz in (-1, 1, 0) if (dy, dz) != (0, 0)
 ]
@@ -713,14 +713,14 @@
             send(fy.at[k, 0], ry.at[k, 1], at_y(-1)),
             send(fy.at[k, 1], ry.at[k, 0], at_y(1)),
         ]
-        if with_mass and k == 1:
-            finish_penalty()
         if k == 1:
             far[:] = [
                 send(fx.at[k, 0], rx2.at[1, 1], at_x(-2)),
                 send(fx.at[k, 1], rx2.at[0, 1], at_x(2)),
             ]
         rest = z_line(parts, zmat)
+        if with_mass and k == 1:
+            finish_penalty()
         if with_mass:
             rest = rest + pav[...] * vx[...]
         tt[...] += rest

time: 51.3 us -> 51.2 us (level)
  no operation moved by 1% of the time
where the time goes in v6:
time: 51.2 us; the launch traced here: 51.1 us
  Pallas kernels  50.4 us (98%)
  between operations  0.64 us (1%)
    pallas_call x1, Pallas kernels, per_device(): pl.pallas_call(kernel, out_shape=shapes, in_specs=[any_spec] * 6, out_spe...  48.6 us
    pallas_call x1, Pallas kernels, per_device(): pl.pallas_call(hand_on, out_shape=shapes, in_specs=[any_spec] * 2, out_sp...  1.82 us

profile of v6, /device:TPU:1, one launch (start us, length us, event | category | flops | bytes accessed | tf_op | source)
XLA Modules:
  0.0 51.1 jit_solution(5155800420954344579)
XLA Ops:
  0.6 48.6 %adjoint.1 = (f32[3,8,32,128]{3,2,1,0:T(8,128)}, f32[8,32,128]{2,1,0:T(8,128)}) custom-call(f32[3,8,32,128]{3,2,1,0:T(8,128)} %base.1, f32[3,8,32,128]{3,2,1,0:T(8,128)} %adj.1, f32[8,32,128]{2,1,0:T(8,128)} %pen.1, bf16[3,256,384]{2,1,0:T(8,128)(2,1)} %constant.6.clone.zblocks, bf16[144,128]{1,0:T(8,128)(2,1)} %constant.7.clone.zfaces, ...), custom_call_target="tpu_custom_call" | custom-call | tf_op jit(solution)/shard_map/adjoint/pallas_call | solution.py:933
  49.3 1.8 %hand_on.1 = (f32[3,8,32,128]{3,2,1,0:T(8,128)}, f32[8,32,128]{2,1,0:T(8,128)}) custom-call(f32[3,8,32,128]{3,2,1,0:T(8,128)} %get-tuple-element.4.projected_in, f32[8,32,128]{2,1,0:T(8,128)} %get-tuple-element.5.pressure_in), custom_call_target="tpu_custom_call" | custom-call | tf_op jit(solution)/shard_map/hand_on/pallas_call | solution.py:996
